TPU v7x, 32 devices: a whole 2x2x4 slice. The times are simulated.
32 devices in a mesh: grp: 2 (over x), lat: 16 (over z, y, core).
Axes of the slice: x: 2, y: 2, z: 4, core: 2. Of those that a mesh axis runs over, the one named last changes fastest.
Arguments:
- fields: bfloat16 [2, 32, 128, 384], P('grp', 'lat'), may hold values from -6 to 6
- cotangent: bfloat16 [2, 32, 128, 384], P('grp', 'lat'), may hold values from -6 to 6
- ocean_kernels: bfloat16 [2, 3, 3, 192, 192], replicated, may hold values from -0.15625 to 0.15625
- atmos_kernels: bfloat16 [2, 3, 3, 384, 384], replicated, may hold values from -0.109375 to 0.109375
- ocean_surface: bfloat16 [192, 4], replicated, may hold values from -0.4375 to 0.4375
- ocean_coupling: bfloat16 [4, 192], replicated, may hold values from -3 to 3
- atmos_flux: bfloat16 [384, 4], replicated, may hold values from -0.3125 to 0.3125
- atmos_coupling: bfloat16 [4, 384], replicated, may hold values from -3 to 3
- row_map: int32 [32], P('lat'), may hold values from 0 to 31, as said below
- wet_mask: int32 [32, 256], P('lat'), may hold values 0 or 1
Outputs:
- next_fields: bfloat16 [2, 32, 128, 384], P('grp', 'lat')
- field_grads: bfloat16 [2, 32, 128, 384], P('grp', 'lat')
- ocean_kernel_grad: float32 [663552], P(('grp', 'lat'))
- atmos_kernel_grad: float32 [2654208], P(('grp', 'lat'))
Inputs may be any that keep to these rules, and one draw needn't show every extreme that they name: row_map never falls, keeps each ocean row in its own band of 2 rows, and maps the first and last row of every band to that band's first and last row.
All inputs are finite; a program needn't handle non-finite values. No bound on the sum of `wet_mask` on one device may be relied on, other than what follows from the above.
Results may differ from a plain program's by a relative error of at most 0.0065.
Values may be sent and summed in bfloat16 or wider, within the bound.
No kernel may reach another device: no remote copies, remote signals or barrier semaphores. Data moves between devices by JAX's collectives and lax.ppermute only.
A program may use at most 128 MiB of HBM per device.

v0:
```python
import functools
import math

import jax
import jax.numpy as jnp
from jax import lax
from jax.experimental import pallas as pl
from jax.experimental.pallas import tpu as pltpu
from jax.sharding import PartitionSpec as P

HIGHEST = lax.Precision.HIGHEST
GELU_SCALE = 0.7978845608028654
GELU_CUBIC = 0.044715
F32 = jnp.float32
BF16 = jnp.bfloat16
WHOLE = pl.BlockSpec(memory_space=pltpu.VMEM)
IN_PLACE = pl.BlockSpec(memory_space=pltpu.HBM)
ANYWHERE = pl.BlockSpec(memory_space=pl.ANY)
VMEM_LIMIT = 20 * 1024 * 1024
PACE = 8
PACK_VMEM = 62 * 1024 * 1024
HOLD_VMEM = 42 * 1024 * 1024

NN = (((1,), (0,)), ((), ()))
NT = (((1,), (1,)), ((), ()))
TN = (((0,), (0,)), ((), ()))


def shape(dims, kind):
    return jax.ShapeDtypeStruct(dims, kind)


def call(kernel, outs, inputs, in_specs=None, scratch=(), flops=0, moved=0, name=None, limit=VMEM_LIMIT, out_spec=WHOLE):
    return pl.pallas_call(
        kernel,
        out_shape=outs,
        in_specs=in_specs or [WHOLE] * len(inputs),
        out_specs=jax.tree.map(lambda _: out_spec, outs),
        scratch_shapes=list(scratch),
        compiler_params=pltpu.CompilerParams(vmem_limit_bytes=limit),
        cost_estimate=pl.CostEstimate(flops=flops, bytes_accessed=moved, transcendentals=0),
        name=name,
    )(*inputs)


def on_ocean():
    return lax.axis_index("grp") == 0


def dot(left, right, dims=NN, precision=None):
    return lax.dot_general(left, right, dims, precision=precision, preferred_element_type=F32)


def moved_cells(values, axis, cols):
    count = values.shape[axis]
    place = lax.rem(lax.broadcasted_iota(jnp.int32, values.shape, axis), cols)
    before = jnp.where(place == 0, 0.0, pltpu.roll(values, 1, axis))
    after = jnp.where(place == cols - 1, 0.0, pltpu.roll(values, count - 1, axis))
    return before, after


def wet_halves(wet, cols, channels):
    source = lax.broadcasted_iota(jnp.int32, (2 * cols, 2 * cols), 0)
    target = lax.broadcasted_iota(jnp.int32, (2 * cols, 2 * cols), 1)
    wanted = 2 * lax.rem(target, cols) + jnp.where(target >= cols, 1, 0)
    chooser = (source == wanted).astype(F32).astype(BF16)
    padded = jnp.concatenate([wet.astype(F32), jnp.zeros((14, 2 * cols), F32)], axis=0)
    apart = dot(padded.astype(BF16), chooser)
    return jnp.concatenate([apart, jnp.zeros((16, channels - 2 * cols), F32)], axis=1)


def own_bit(bit):
    return lax.rem(lax.shift_right_logical(lax.axis_index("lat"), bit), 2)


def pack_kernel(
    x_any, g_any, wet_any, near_ref, far_ref, early_ref, own_ref, x_ref, g_ref, wet_ref, sems, *, cols
):
    pairs = ((wet_any, wet_ref), (x_any, x_ref), (g_any, g_ref))
    copies = [pltpu.make_async_copy(*pair, sems.at[index]) for index, pair in enumerate(pairs)]
    for copy in copies:
        copy.start()
    core = own_bit(0)
    copies[0].wait()
    wide = wet_halves(wet_ref[...], cols, x_ref.shape[2])
    other = pltpu.roll(wide, 15, 0)
    own_ref[4 * cols :, :] = wide.astype(BF16)
    far_ref[2 * cols :, :] = jnp.where(core == 0, wide, other).astype(BF16)
    near_ref[2 * cols :, :] = jnp.where(core == 0, other, wide).astype(BF16)
    copies[1].wait()
    copies[2].wait()
    for part, ref in enumerate((x_ref, g_ref)):
        far_ref[part * cols : (part + 1) * cols, :] = ref[core]
        near_ref[part * cols : (part + 1) * cols, :] = ref[1 - core]
        own_ref[2 * part * cols : (2 * part + 1) * cols, :] = ref[0]
        own_ref[(2 * part + 1) * cols : (2 * part + 2) * cols, :] = ref[1]
    for row in range(2):
        early_ref[row * cols : (row + 1) * cols, :] = jnp.where(on_ocean(), g_ref[row], x_ref[row])


def hold_kernel(own_in, atmos_any, ocean_any, own_ref, atmos_ref, ocean_ref, sem):
    narrow = ocean_ref.shape[2]
    ocean_copy = pltpu.make_async_copy(ocean_any, ocean_ref.at[:, pl.ds(0, narrow), :], sem)
    atmos_copy = pltpu.make_async_copy(atmos_any, atmos_ref, sem)

    @pl.when(on_ocean())
    def _():
        ocean_copy.start()
        gap = ocean_ref.shape[1] - narrow
        if gap:
            ocean_ref[:, narrow:, :] = jnp.zeros((ocean_ref.shape[0], gap, narrow), BF16)

    @pl.when(jnp.logical_not(on_ocean()))
    def _():
        atmos_copy.start()

    own_ref[...] = own_in[...]

    @pl.when(on_ocean())
    def _():
        ocean_copy.wait()

    @pl.when(jnp.logical_not(on_ocean()))
    def _():
        atmos_copy.wait()


def low_and_high(near, far):
    core = own_bit(0)
    return jnp.where(core == 0, far, near), jnp.where(core == 0, near, far)


def outgoing_kernel(
    own_ref, near_ref, far_ref, terms_ref, xpad_ref, gpad_ref, wet_ref, edge_ref, sent_ref, *, cols
):
    low, high = low_and_high(near_ref[...], far_ref[...])
    for part, pad_ref in enumerate((xpad_ref, gpad_ref)):
        pad_ref[0:cols, :] = low[part * cols : (part + 1) * cols]
        pad_ref[cols : 3 * cols, :] = own_ref[2 * part * cols : 2 * (part + 1) * cols, :]
        pad_ref[3 * cols : 4 * cols, :] = high[part * cols : (part + 1) * cols]
    low_wet = low[2 * cols :].astype(F32)
    high_wet = high[2 * cols :].astype(F32)
    own_wet = own_ref[4 * cols :, :].astype(F32)
    halves = []
    for start in (0, cols):
        lanes = slice(start, start + cols)
        rows = (low_wet[0:1, lanes], own_wet[0:1, lanes], own_wet[1:2, lanes], high_wet[0:1, lanes])
        halves.append(jnp.concatenate(rows, axis=1))
    first_wet, second_wet = halves
    inverse = 1.0 / jnp.maximum(first_wet + second_wet, 1.0)
    wet_ref[0:1, :] = first_wet
    wet_ref[1:2, :] = second_wet
    wet_ref[2:3, :] = inverse
    wet_ref[3:8, :] = jnp.zeros((5, 4 * cols), F32)
    xpad = xpad_ref[...]
    projected = dot(terms_ref[0:8, :].astype(BF16), xpad, NT)
    mixed = (projected[0:4] * first_wet + projected[4:8] * second_wet) * inverse
    sent_ref[...] = jnp.where(on_ocean(), mixed, projected[0:4])
    edge_ref[0:cols, :] = jnp.where(on_ocean(), gpad_ref[0:cols, :], xpad_ref[0:cols, :])
    edge_ref[cols:, :] = jnp.where(on_ocean(), gpad_ref[3 * cols :, :], xpad_ref[3 * cols :, :])


def halves_apart(values, narrow):
    wide = -(-narrow // 128) * 128
    lane = lax.broadcasted_iota(jnp.int32, values.shape, 1)
    even = jnp.where(lane < narrow, values, 0.0)
    odd = jnp.where(lane < narrow, pltpu.roll(values, narrow, 1), 0.0)
    return even[:, :wide], odd[:, :wide]


def halves_with_columns(pad, cols):
    even, odd = halves_apart(pad.astype(F32), pad.shape[1] // 2)
    odd_before = moved_cells(odd, 0, cols)[0].astype(BF16)
    even_after = moved_cells(even, 0, cols)[1].astype(BF16)
    even, odd = even.astype(BF16), odd.astype(BF16)
    return (odd_before, even, odd), (even, odd, even_after)


def with_columns(pad, cols):
    before, after = moved_cells(pad.astype(F32), 0, cols)
    return before.astype(BF16), pad, after.astype(BF16)


def convolve(pad, out_ref, atmos_ref, ocean_ref, layer, flipped, cols):
    base = 9 * layer
    channels = atmos_ref.shape[2]
    wide, narrow = ocean_ref.shape[1:]
    rows = out_ref.shape[0]

    def summed(pick):
        total = None
        for row_tap in range(3):
            part = pick(row_tap, slice(cols * row_tap, cols * row_tap + rows))
            total = part if total is None else total + part
        return total

    @pl.when(on_ocean())
    def _():
        evens, odds = halves_with_columns(pad, cols)
        if flipped:

            def pick(row_tap, span):
                part = None
                for col_tap in range(3):
                    left = jnp.concatenate([evens[col_tap][span], odds[col_tap][span]], axis=0)
                    kernel = ocean_ref[base + 8 - (3 * row_tap + col_tap), 0:narrow, :]
                    piece = dot(left[:, :narrow], kernel, NT)
                    part = piece if part is None else part + piece
                return part

        else:
            even, odd = jnp.concatenate(evens, axis=1), jnp.concatenate(odds, axis=1)

            def pick(row_tap, span):
                first = base + 3 * row_tap
                kernel = ocean_ref[first : first + 3].reshape(3 * wide, narrow)
                return dot(jnp.concatenate([even[span], odd[span]], axis=0), kernel)

        total = summed(pick)
        out_ref[...] = jnp.concatenate([total[:rows], total[rows:]], axis=1)

    @pl.when(jnp.logical_not(on_ocean()))
    def _():
        taps = with_columns(pad, cols)
        if flipped:

            def pick(row_tap, span):
                part = None
                for col_tap in range(3):
                    piece = dot(taps[col_tap][span], atmos_ref[base + 8 - (3 * row_tap + col_tap)], NT)
                    part = piece if part is None else part + piece
                return part

        else:
            joined = jnp.concatenate(taps, axis=1)

            def pick(row_tap, span):
                first = base + 3 * row_tap
                return dot(joined[span], atmos_ref[first : first + 3].reshape(3 * channels, channels))

        out_ref[...] = summed(pick)


def back_kernel(gpad_ref, atmos_ref, ocean_ref, out_ref, *, cols):
    convolve(gpad_ref[...], out_ref, atmos_ref, ocean_ref, 1, True, cols)


def spread(arrived, wet, mixing, terms):
    first_wet, second_wet = wet
    both = jnp.concatenate([arrived * first_wet, arrived * second_wet], axis=0)
    alone = jnp.concatenate([arrived, jnp.zeros_like(arrived)], axis=0)
    return dot(jnp.where(mixing, both, alone), terms, TN, HIGHEST)


def first_kernel(
    xpad_ref, wet_ref, arrived_ref, terms_ref, back_ref, atmos_ref, ocean_ref,
    u_ref, stay_ref, give_ref, near_ref, far_ref, first_ref, *, cols,
):
    wet = wet_ref[0:1, :], wet_ref[1:2, :]
    coupled = spread(arrived_ref[...], wet, on_ocean(), terms_ref[8:16, :])
    u = (xpad_ref[...].astype(F32) + coupled).astype(BF16)
    u_ref[...] = u
    convolve(u, first_ref, atmos_ref, ocean_ref, 0, False, cols)
    first = first_ref[...]
    tangent = jnp.tanh(GELU_SCALE * (first + GELU_CUBIC * first * first * first))
    hidden = (0.5 * first * (1.0 + tangent)).astype(BF16)
    slope = 0.5 * (1.0 + tangent) + 0.5 * first * (1.0 - tangent * tangent) * GELU_SCALE * (
        1.0 + 3.0 * GELU_CUBIC * first * first
    )
    first_grad = (back_ref[...] * slope).astype(BF16)
    stay_ref[...] = jnp.where(on_ocean(), first_grad, hidden)
    give_ref[...] = jnp.where(on_ocean(), hidden, first_grad)
    core = own_bit(0)
    for part, values in enumerate((hidden, first_grad)):
        target = slice(part * cols, (part + 1) * cols)
        far_ref[target, :] = jnp.where(core == 0, values[:cols], values[cols:])
        near_ref[target, :] = jnp.where(core == 0, values[cols:], values[:cols])


def whole_pad(early_ref, edge_ref, cols):
    parts = [edge_ref[0:cols, :], early_ref[...], edge_ref[cols:, :]]
    return jnp.concatenate(parts, axis=0).astype(F32)


def grad_atmos(pad, own, cols, store):
    rows = own.shape[0]
    left = own.T.astype(BF16)
    before, after = moved_cells(pad, 0, cols)
    rights = [part.astype(BF16) for part in (after, pad, before)]
    for tap in range(9):
        start = cols * (2 - tap // 3)
        store(tap, dot(left, rights[tap % 3][start : start + rows]))


def grad_ocean(pad, own, pad_is_input, cols, store):
    rows, channels = own.shape
    narrow = channels // 2

    if pad_is_input:
        middle = pad.T
        before, after = moved_cells(middle, 1, cols)
        even, odd = middle[:narrow].astype(BF16), middle[narrow:].astype(BF16)
        pairs = (
            (before[narrow:].astype(BF16), even),
            (even, odd),
            (odd, after[:narrow].astype(BF16)),
        )
        right = jnp.concatenate(halves_apart(own, narrow), axis=0).astype(BF16)
        for tap in range(9):
            start = cols * (tap // 3)
            pieces = [part[:, start : start + rows] for part in pairs[tap % 3]]
            store(tap, dot(jnp.concatenate(pieces, axis=1), right))
    else:
        turned = own.T.astype(BF16)
        left = jnp.concatenate([turned[:narrow], turned[narrow:]], axis=1)
        even, odd = halves_apart(pad, narrow)
        odd_before = moved_cells(odd, 0, cols)[0].astype(BF16)
        even_after = moved_cells(even, 0, cols)[1].astype(BF16)
        even, odd = even.astype(BF16), odd.astype(BF16)
        pairs = ((odd, even_after), (even, odd), (odd_before, even))
        for tap in range(9):
            start = cols * (2 - tap // 3)
            pieces = [part[start : start + rows] for part in pairs[tap % 3]]
            store(tap, dot(left, jnp.concatenate(pieces, axis=0)))


def store_into(out_ref):
    def store(tap, value):
        if len(out_ref.shape) == 2:
            rows = value.shape[0]
            out_ref[rows * tap : rows * (tap + 1), :] = value
        else:
            rows = value.shape[0]
            for piece in range(out_ref.shape[0]):
                lanes = slice(128 * piece, 128 * (piece + 1))
                out_ref[piece, rows * tap : rows * (tap + 1), :] = value[:, lanes]

    return store


def hidden_and_grad(stay_ref, give_ref):
    stay, give = stay_ref[...], give_ref[...]
    return jnp.where(on_ocean(), give, stay), jnp.where(on_ocean(), stay, give)


def shifted_inputs(pad, cols):
    middle = pad.T
    before, after = moved_cells(middle, 1, cols)
    return [part.astype(BF16) for part in (before, middle, after)]


def own_grads_kernel(
    upad_ref, gpad_ref, stay_ref, early_ref, edge_ref, sent_ref, coupling_ref,
    atmos_out, ocean_out, left_ref, *, cols,
):
    stay = stay_ref[...].astype(F32)

    @pl.when(on_ocean())
    def _():
        grad_ocean(upad_ref[...].astype(F32), stay, True, cols, store_into(ocean_out))
        added = dot(sent_ref[...], coupling_ref[...].astype(F32), TN, HIGHEST)
        other = (whole_pad(early_ref, edge_ref, cols) + added).astype(BF16).astype(F32)
        for tap, left in enumerate(shifted_inputs(other, cols)):
            left_ref[tap] = left

    @pl.when(jnp.logical_not(on_ocean()))
    def _():
        grad_atmos(gpad_ref[...].astype(F32), stay, cols, store_into(atmos_out))


def other_grads_kernel(left_ref, late_ref, early_ref, edge_ref, atmos_out, ocean_out, *, cols):
    rows = late_ref.shape[0]

    @pl.when(on_ocean())
    def _():
        store = store_into(atmos_out)
        for tap in range(9):
            start = cols * (tap // 3)
            store(tap, dot(left_ref[tap % 3, :, start : start + rows], late_ref[...]))

    @pl.when(jnp.logical_not(on_ocean()))
    def _():
        late = late_ref[...].astype(F32)
        grad_ocean(whole_pad(early_ref, edge_ref, cols), late, False, cols, store_into(ocean_out))


def chunk_rows(keep_ref, send_ref, atmos_all, ocean_all, chunks):
    channels = keep_ref.shape[2]
    pieces = ocean_all.shape[0]
    atmos_rows = atmos_all.shape[0] // chunks
    ocean_rows = atmos_rows // 2
    taken = keep_ref.shape[1] - atmos_rows
    core = lax.rem(lax.axis_index("lat"), 2)
    blank = jnp.zeros((taken, channels - 128 * pieces), F32)
    for out_ref, side in ((send_ref, 1 - core), (keep_ref, core)):
        for pair in range(chunks // 2):
            start = pl.multiple_of(atmos_rows * (2 * pair + side), 8)
            upper = atmos_all[pl.ds(start, atmos_rows), :]
            start = ocean_rows * (2 * pair + side)
            halves = []
            for odd in range(2):
                parts = [ocean_all.at[piece][pl.ds(start + odd, taken, 2), :] for piece in range(pieces)]
                halves.append(jnp.concatenate(parts + [blank], axis=1))
            lower = halves[0] + pltpu.roll(halves[1], channels // 2, 1)
            out_ref[pair] = jnp.concatenate([upper, lower], axis=0).astype(BF16)


def chunk_kernel(
    atmos_own, ocean_own, atmos_other, ocean_other, near_any, far_any, keep_ref, send_ref, *, chunks
):
    @pl.when(on_ocean())
    def _():
        chunk_rows(keep_ref, send_ref, atmos_other, ocean_own, chunks)

    @pl.when(jnp.logical_not(on_ocean()))
    def _():
        chunk_rows(keep_ref, send_ref, atmos_own, ocean_other, chunks)


def halve(keep_ref, came_ref, keep_out, send_out, bit, rows):
    own = own_bit(bit)
    for out_ref, side in ((send_out, 1 - own), (keep_out, own)):
        for outer in range(keep_ref.shape[0]):
            for inner in range(keep_ref.shape[2]):
                total = keep_ref[outer, side, inner, rows, :].astype(F32)
                total = total + came_ref[outer, side, inner, rows, :].astype(F32)
                out_ref[outer, inner] = total.astype(BF16)


def split_kernel(keep_ref, came_ref, done_ref, *outs, cuts):
    by_z = [ref.reshape(2, 2, 2, *keep_ref.shape[3:]) for ref in (keep_ref, came_ref)]
    start = 0
    for index, rows in enumerate(cuts):
        refs, bit = (by_z, 2) if index == 1 else ((keep_ref, came_ref), 1)
        halve(*refs, *outs[2 * index : 2 * index + 2], bit, slice(start, start + rows))
        start += rows


def halve_kernel(keep_ref, came_ref, *refs, bit):
    keep_out, send_out, mark_ref = refs[-3:]
    halve(keep_ref, came_ref, keep_out, send_out, bit, slice(None))
    mark_ref[...] = jnp.zeros_like(mark_ref)


MARK = shape((8, 128), F32)


def halved(keep, came, bit, dims, after):
    outer, inner, rows, channels = dims[0], dims[1], keep.shape[-2], keep.shape[-1]
    keep, came = (part.reshape(outer, 2, inner, rows, channels) for part in (keep, came))
    out = shape((outer, inner, rows, channels), BF16)
    return call(
        functools.partial(halve_kernel, bit=bit),
        [out, out, MARK],
        [keep, came, *after],
        [WHOLE] * 2 + [ANYWHERE] * len(after),
        moved=8 * outer * inner * rows * channels,
        name="halve",
    )


def scatter_sum(keep, came, done_before, done_next):
    pairs, tall, channels = keep.shape
    cuts = [16 * (tall // 16 * part // 17) for part in (6, 6)]
    cuts.append(tall - sum(cuts))
    outs = []
    for index, rows in enumerate(cuts):
        outs += [shape(((2, 2) if index == 1 else (4, 1)) + (rows, channels), BF16)] * 2
    keep, came = (part.reshape(4, 2, 1, tall, channels) for part in (keep, came))
    parts = call(
        functools.partial(split_kernel, cuts=cuts),
        outs,
        [keep, came, done_before],
        [WHOLE] * 2 + [ANYWHERE],
        moved=6 * pairs * tall * channels,
        name="split",
    )
    a_keep, a_send, b_keep, b_send, c_keep, c_send = parts
    a_came = swapped(a_send, "lat", 2)
    b_came = swapped(b_send, "lat", 4)
    c_came = swapped(c_send, "lat", 2)
    a_keep, a_send, mark = halved(a_keep, a_came, 2, (2, 1), done_next)
    a_came = swapped(a_send, "lat", 4)
    b_keep, b_send, mark = halved(b_keep, b_came, 3, (1, 2), [mark])
    b_came = swapped(b_send, "lat", 8)
    c_keep, c_send, mark = halved(c_keep, c_came, 2, (2, 1), [mark])
    c_came = swapped(c_send, "lat", 4)
    a_keep, a_send, mark = halved(a_keep, a_came, 3, (1, 1), [mark])
    a_came = swapped(a_send, "lat", 8)
    b_keep, b_send, mark = halved(b_keep, b_came, 1, (1, 1), [mark])
    b_came = swapped(b_send, "lat", 2)
    c_keep, c_send, mark = halved(c_keep, c_came, 3, (1, 1), [mark])
    c_came = swapped(c_send, "lat", 8)
    return [part.reshape(-1, channels) for part in (a_keep, a_came, b_keep, b_came, c_keep, c_came)]


def finish_kernel(*refs, atmos_factor, ocean_factor):
    parts, (atmos_ref, ocean_ref) = refs[:-2], refs[-2:]
    channels = parts[0].shape[1]
    pieces = channels // 128
    atmos_rows = atmos_ref.shape[0] // pieces
    ocean_rows = ocean_ref.shape[0] // pieces
    sums = [
        parts[index][...].astype(F32) + parts[index + 1][...].astype(F32)
        for index in range(0, len(parts), 2)
    ]
    total = jnp.concatenate(sums, axis=0)
    for piece in range(pieces):
        lanes = slice(128 * piece, 128 * (piece + 1))
        atmos_ref[pl.ds(piece, atmos_rows, pieces), :] = total[:atmos_rows, lanes] * atmos_factor
        ocean_ref[pl.ds(piece, ocean_rows, pieces), :] = (
            total[atmos_rows : atmos_rows + ocean_rows, lanes] * ocean_factor
        )


def input_grad_kernel(
    stay_ref, give_ref, near_ref, far_ref, gpad_ref, wet_ref, terms_ref, atmos_ref, ocean_ref,
    grad_ref, sent_ref, *, cols,
):
    middle = hidden_and_grad(stay_ref, give_ref)[1]
    low, high = low_and_high(near_ref[cols:, :], far_ref[cols:, :])
    pad = jnp.concatenate([low, middle, high], axis=0)
    own = slice(cols, 3 * cols)
    convolve(pad, grad_ref, atmos_ref, ocean_ref, 0, True, cols)
    grad = gpad_ref[own, :].astype(F32) + grad_ref[...]
    grad_ref[...] = grad
    weighted = dot(terms_ref[8:16, :], grad, NT, HIGHEST)
    mixed = weighted[0:4] * wet_ref[0:1, own] + weighted[4:8] * wet_ref[1:2, own]
    sent_ref[...] = jnp.where(on_ocean(), mixed, weighted[0:4])


def next_kernel(
    stay_ref, give_ref, near_ref, far_ref, upad_ref, atmos_ref, ocean_ref,
    next_ref, mark_ref, second_ref, *, cols,
):
    middle = hidden_and_grad(stay_ref, give_ref)[0]
    low, high = low_and_high(near_ref[0:cols, :], far_ref[0:cols, :])
    pad = jnp.concatenate([low, middle, high], axis=0)
    own = slice(cols, 3 * cols)
    convolve(pad, second_ref, atmos_ref, ocean_ref, 1, False, cols)
    values = (upad_ref[own, :].astype(F32) + second_ref[...]).astype(BF16)
    next_ref[0] = values[:cols]
    next_ref[1] = values[cols:]
    mark_ref[...] = jnp.zeros_like(mark_ref)


def last_kernel(grad_ref, arrived_ref, wet_ref, terms_ref, out_ref, mark_ref, *, cols):
    own = slice(cols, 3 * cols)
    wet = wet_ref[0:1, own], wet_ref[1:2, own]
    arrived = jnp.where(on_ocean(), arrived_ref[...] * wet_ref[2:3, own], arrived_ref[...])
    added = spread(arrived, wet, on_ocean(), terms_ref[0:8, :])
    values = (grad_ref[...] + added).astype(BF16)
    out_ref[0] = values[:cols]
    out_ref[1] = values[cols:]
    mark_ref[...] = jnp.zeros_like(mark_ref)


def swapped(value, axis, mask):
    pairs = [(source, source ^ mask) for source in range(lax.axis_size(axis))]
    return lax.ppermute(value, axis, pairs)


def halo(near, far):
    count = lax.axis_size("lat")
    pairs = [(i, i + 1 if i % 2 else i - 1) for i in range(1, count - 1)]
    far = lax.ppermute(far, "lat", pairs)
    return swapped(near, "lat", 1), far


def local(
    fields,
    cotangent,
    ocean_kernels,
    atmos_kernels,
    ocean_surface,
    ocean_coupling,
    atmos_flux,
    atmos_coupling,
    row_map,
    wet_mask,
):
    x, g = fields[0], cotangent[0]
    bands, cols, channels = x.shape
    narrow = channels // 2
    cells = bands * cols
    count = lax.axis_size("lat")
    is_ocean = lax.axis_index("grp") == 0
    atmos_factor = 1.0 / math.sqrt(bands * count * cols)
    ocean_factor = 1.0 / math.sqrt(bands * count * 2 * cols)
    bound = functools.partial

    blank = jnp.zeros((4, narrow), BF16)
    gap = jnp.zeros((4, channels), BF16)
    surface = ocean_surface.T
    ocean_terms = jnp.concatenate(
        [
            jnp.concatenate([surface, blank], axis=1),
            jnp.concatenate([blank, surface], axis=1),
            jnp.concatenate([ocean_coupling, blank], axis=1),
            jnp.concatenate([blank, ocean_coupling], axis=1),
        ],
        axis=0,
    )
    atmos_terms = jnp.concatenate([atmos_flux.T, gap, atmos_coupling, gap], axis=0)
    terms = jnp.where(is_ocean, ocean_terms, atmos_terms).astype(F32)

    edge = shape((2 * cols + 16, channels), BF16)
    half = shape((cells, channels), BF16)
    near, far, own_early, own = call(
        bound(pack_kernel, cols=cols),
        [edge, edge, half, shape((2 * cells + 16, channels), BF16)],
        [x, g, wet_mask],
        [IN_PLACE] * 3,
        [
            pltpu.VMEM(x.shape, BF16),
            pltpu.VMEM(x.shape, BF16),
            pltpu.VMEM(wet_mask.shape, jnp.int32),
            pltpu.SemaphoreType.DMA((3,)),
        ],
        name="pack",
        limit=PACK_VMEM,
    )
    near, far = halo(near, far)
    other_early = swapped(own_early, "grp", 1)
    wide = -(-narrow // 128) * 128
    own, atmos_flat, ocean_flat = call(
        hold_kernel,
        [
            shape(own.shape, BF16),
            shape((18, channels, channels), BF16),
            shape((18, wide, narrow), BF16),
        ],
        [own, atmos_kernels.reshape(18, channels, channels), ocean_kernels.reshape(18, narrow, narrow)],
        [WHOLE, IN_PLACE, IN_PLACE],
        [pltpu.SemaphoreType.DMA],
        flops=PACE * 10**8,
        name="hold",
        limit=HOLD_VMEM,
    )
    pad = shape((2 * cells, channels), BF16)
    xpad, gpad, wet, edges, sent = call(
        bound(outgoing_kernel, cols=cols),
        [pad, pad, shape((8, 2 * cells), F32), half, shape((4, 2 * cells), F32)],
        [own, near, far, terms],
        name="outgoing",
    )
    arrived = swapped(sent, "grp", 1)
    other_edges = swapped(edges, "grp", 1)
    conv_cost = dict(flops=PACE * 9 * cells * channels * channels, moved=9 * channels * channels * 2)
    back = call(
        bound(back_kernel, cols=cols),
        shape((cells, channels), F32),
        [gpad, atmos_flat, ocean_flat],
        **conv_cost,
        name="back",
    )
    upad, stay, give, near, far = call(
        bound(first_kernel, cols=cols),
        [pad, half, half, half, half],
        [xpad, wet, arrived, terms, back, atmos_flat, ocean_flat],
        None,
        [pltpu.VMEM((cells, channels), F32)],
        **conv_cost,
        name="first",
    )
    late = swapped(give, "grp", 1)

    near, far = halo(near, far)

    atmos_rows = 9 * channels // count
    ocean_rows = 9 * narrow // count
    chunked = count == 16 and 9 * channels % (8 * count) == 0 and ocean_rows % 2 == 0
    tall = -(-(atmos_rows + ocean_rows // 2) // 16) * 16
    spare = max(0, 2 * (tall - atmos_rows) - ocean_rows) if chunked else 0
    ocean_tall = 9 * narrow + -(-spare // 8) * 8
    sums = [shape((9 * channels, channels), F32), shape((wide // 128, ocean_tall, 128), F32)]
    atmos_sum, ocean_sum, lefts = call(
        bound(own_grads_kernel, cols=cols),
        [*sums, shape((3, channels, 2 * cells), BF16)],
        [upad, gpad, stay, other_early, other_edges, sent, atmos_coupling],
        **conv_cost,
        name="own_grads",
    )
    atmos_other, ocean_other = call(
        bound(other_grads_kernel, cols=cols),
        sums,
        [lefts, late, other_early, other_edges],
        **conv_cost,
        name="other_grads",
    )
    if chunked:
        part = shape((count // 2, tall, channels), BF16)
        keep, send = call(
            bound(chunk_kernel, chunks=count),
            [part, part],
            [atmos_sum, ocean_sum, atmos_other, ocean_other, near, far],
            [WHOLE] * 4 + [ANYWHERE] * 2,
            moved=4 * count * tall * channels,
            name="chunk",
        )
        came = swapped(send, "lat", 1)

    grad, sent_back = call(
        bound(input_grad_kernel, cols=cols),
        [shape((cells, channels), F32), shape((4, cells), F32)],
        [stay, give, near, far, gpad, wet, terms, atmos_flat, ocean_flat],
        **conv_cost,
        name="input_grad",
    )
    returned = swapped(sent_back, "grp", 1)
    next_field, next_mark = call(
        bound(next_kernel, cols=cols),
        [shape(x.shape, BF16), MARK],
        [stay, give, near, far, upad, atmos_flat, ocean_flat],
        None,
        [pltpu.VMEM((cells, channels), F32)],
        **conv_cost,
        name="next",
    )
    field_grad, last_mark = call(
        bound(last_kernel, cols=cols),
        [shape(x.shape, BF16), MARK],
        [grad, returned, wet, terms],
        name="last",
    )

    if chunked:
        atmos_chunk, ocean_chunk = call(
            bound(finish_kernel, atmos_factor=atmos_factor, ocean_factor=ocean_factor),
            [
                shape((atmos_rows * channels // 128, 128), F32),
                shape((ocean_rows * narrow // 128, 128), F32),
            ],
            scatter_sum(keep, came, sent_back, [next_mark, last_mark]),
            name="finish",
        )
        atmos_total, ocean_total = atmos_chunk.reshape(-1), ocean_chunk.reshape(-1)
    else:
        atmos_all = jnp.where(is_ocean, atmos_other, atmos_sum)
        ocean_all = jnp.where(is_ocean, ocean_sum, ocean_other)
        atmos_total = atmos_factor * lax.psum_scatter(
            atmos_all.reshape(-1), "lat", scatter_dimension=0, tiled=True
        )
        ocean_all = jnp.concatenate([ocean_all[piece] for piece in range(wide // 128)], axis=1)
        ocean_total = ocean_factor * lax.psum_scatter(
            ocean_all[:, :narrow].reshape(-1), "lat", scatter_dimension=0, tiled=True
        )
    return (next_field[None], field_grad[None], ocean_total, atmos_total)


def solution(mesh):
    in_specs = (
        P("grp", "lat", None, None),
        P("grp", "lat", None, None),
        P(),
        P(),
        P(),
        P(),
        P(),
        P(),
        P("lat"),
        P("lat", None),
    )
    out_specs = (
        P("grp", "lat", None, None),
        P("grp", "lat", None, None),
        P(("grp", "lat")),
        P(("grp", "lat")),
    )
    return jax.shard_map(local, mesh=mesh, in_specs=in_specs, out_specs=out_specs, check_vma=False)
```

profile of v0, /device:TPU:0, one launch (start us, length us, event | category | flops | bytes accessed | tf_op | source)
XLA Modules:
  0.0 65.6 jit_solution(5375419601798341296)
XLA Ops:
  0.6 2.0 %pack.1 = (bf16[272,384]{1,0:T(8,128)(2,1)}, bf16[272,384]{1,0:T(8,128)(2,1)}, bf16[256,384]{1,0:T(8,128)(2,1)}, bf16[528,384]{1,0:T(8,128)(2,1)}) custom-call(bf16[2,128,384]{2,1,0:T(8,128)(2,1)} %bitcast.56, bf16[2,128,384]{2,1,0:T(8,128)(2,1)} %bitcast.57, s32[2,256]{1,0:T(2,128)} %wet_any.1), custom_call_target="tpu_custom_call" | custom-call | tf_op jit(solution)/shard_map/pack/pallas_call | solution.py:34
  3.9 2.6 %collective-permute-start.6 = (bf16[256,384]{1,0:T(8,128)(2,1)}, bf16[256,384]{1,0:T(8,128)(2,1)S(1)}, u32[]{:S(2)}, u32[]{:S(2)}) collective-permute-start(bf16[256,384]{1,0:T(8,128)(2,1)} %get-tuple-element.78), channel_id=1, source_target_pairs={{0,16},{16,0},{1,17},{17,1},{2,18},{18,2},{3,19},{19,3},{4,20},{20... | collective-permute-start | bytes 589832 | tf_op jit(solution)/shard_map/ppermute | solution.py:560
  6.4 1.5 %copy-done = bf16[2,3,3,192,192]{4,3,2,1,0:T(8,128)(2,1)S(1)} copy-done((bf16[2,3,3,192,192]{4,3,2,1,0:T(8,128)(2,1)S(1)}, bf16[2,3,3,192,192]{4,3,2,1,0:T(8,128)(2,1)}, u32[]{:S(2)}) %copy-start) | copy-done | bytes 1327128
  7.9 1.0 %copy-done.1 = bf16[528,384]{1,0:T(8,128)(2,1)S(1)} copy-done((bf16[528,384]{1,0:T(8,128)(2,1)S(1)}, bf16[528,384]{1,0:T(8,128)(2,1)}, u32[]{:S(2)}) %copy-start.1) | copy-done | bytes 405528
  10.0 2.0 %collective-permute-start.2 = (f32[4,512]{1,0:T(4,128)S(1)}, f32[4,512]{1,0:T(4,128)S(1)}, u32[]{:S(2)}, u32[]{:S(2)}) collective-permute-start(f32[4,512]{1,0:T(4,128)S(1)} %get-tuple-element.65.sent_ref), channel_id=1, source_target_pairs={{0,16},{16,0},{1,17},{17,1},{2,18},{18,2},{3,19},{19,3},{4,20},{20... | collective-permute-start | bytes 24584 | tf_op jit(solution)/shard_map/ppermute | solution.py:560
  12.1 0.9 %back.1.back_ref = f32[256,384]{1,0:T(8,128)S(1)} custom-call(bf16[512,384]{1,0:T(8,128)(2,1)S(1)} %get-tuple-element.66.gpad_ref, bf16[18,384,384]{2,1,0:T(8,128)(2,1)S(1)} %get-tuple-element.67.atmos_ref, bf16[18,256,192]{2,1,0:T(8,128)(2,1)S(1)} %get-tuple-element.68.ocean_ref), custom_call_target="tpu_custom_call" | custom-call | flops 2717908992 | bytes 2654208 | tf_op jit(solution)/shard_map/back/pallas_call | solution.py:34
  13.7 2.1 %first.1 = (bf16[512,384]{1,0:T(8,128)(2,1)S(1)}, bf16[256,384]{1,0:T(8,128)(2,1)S(1)}, bf16[256,384]{1,0:T(8,128)(2,1)S(1)}, bf16[256,384]{1,0:T(8,128)(2,1)S(1)}, bf16[256,384]{1,0:T(8,128)(2,1)S(1)}) custom-call(bf16[512,384]{1,0:T(8,128)(2,1)S(1)} %get-tuple-element.63.xpad_ref, f32[8,512]{1,0:T(8,128)S(1)} %get-tuple-element.64.wet_ref, ...), custom_call_target="tpu_custom_call" | custom-call | flops 2717908992 | bytes 2654208 | tf_op jit(solution)/shard_map/first/pallas_call | solution.py:34
  15.9 2.5 %collective-permute-start.3 = (bf16[256,384]{1,0:T(8,128)(2,1)S(1)}, bf16[256,384]{1,0:T(8,128)(2,1)S(1)}, u32[]{:S(2)}, u32[]{:S(2)}) collective-permute-start(bf16[256,384]{1,0:T(8,128)(2,1)S(1)} %get-tuple-element.71), channel_id=1, source_target_pairs={{0,1},{1,0},{2,3},{3,2},{4,5},{5,4},{6,7},{7,6},{8,9},{9,8},{10,11... | collective-permute-start | bytes 589832 | tf_op jit(solution)/shard_map/ppermute | solution.py:560
  19.1 2.0 %collective-permute-start.8 = (bf16[256,384]{1,0:T(8,128)(2,1)S(1)}, bf16[256,384]{1,0:T(8,128)(2,1)S(1)}, u32[]{:S(2)}, u32[]{:S(2)}) collective-permute-start(bf16[256,384]{1,0:T(8,128)(2,1)S(1)} %get-tuple-element.70.give_ref), channel_id=1, source_target_pairs={{0,16},{16,0},{1,17},{17,1},{2,18},{18,2},{3,19},{19,3},{4,20},{20... | collective-permute-start | bytes 589832 | tf_op jit(solution)/shard_map/ppermute | solution.py:560
  21.1 2.3 %own_grads.1 = (f32[3456,384]{1,0:T(8,128)S(1)}, f32[2,1736,128]{2,1,0:T(8,128)S(1)}, bf16[3,384,512]{2,1,0:T(8,128)(2,1)S(1)}) custom-call(bf16[512,384]{1,0:T(8,128)(2,1)S(1)} %get-tuple-element.73.upad_ref, bf16[512,384]{1,0:T(8,128)(2,1)S(1)} %get-tuple-element.66.gpad_ref, bf16[256,384]{1,0:T(8,128)(2,1)S(1)} %get-tuple-element.69.stay_ref, ...), custom_call_target="tpu_custom_call" | custom-call | flops 2717908992 | bytes 2654208 | tf_op jit(solution)/shard_map/own_grads/pallas_call | solution.py:34
  23.4 1.4 %collective-permute-done.8.late_ref = bf16[256,384]{1,0:T(8,128)(2,1)S(1)} collective-permute-done((bf16[256,384]{1,0:T(8,128)(2,1)S(1)}, bf16[256,384]{1,0:T(8,128)(2,1)S(1)}, u32[]{:S(2)}, u32[]{:S(2)}) %collective-permute-start.8) | collective-permute-done | bytes 196640 | tf_op jit(solution)/shard_map/ppermute | solution.py:560
  24.8 1.1 %other_grads.1 = (f32[3456,384]{1,0:T(8,128)S(1)}, f32[2,1736,128]{2,1,0:T(8,128)S(1)}) custom-call(bf16[3,384,512]{2,1,0:T(8,128)(2,1)S(1)} %get-tuple-element.82.left_ref, bf16[256,384]{1,0:T(8,128)(2,1)S(1)} %collective-permute-done.8.late_ref, bf16[256,384]{1,0:T(8,128)(2,1)S(1)} %collective-permute-done.6.early_ref, ...), custom_call_target="tpu_custom_call" | custom-call | flops 2717908992 | bytes 2654208 | tf_op jit(solution)/shard_map/other_grads/pallas_call | solution.py:34
  25.9 0.8 %chunk.1 = (bf16[8,272,384]{2,1,0:T(8,128)(2,1)S(1)}, bf16[8,272,384]{2,1,0:T(8,128)(2,1)S(1)}) custom-call(f32[3456,384]{1,0:T(8,128)S(1)} %get-tuple-element.80.atmos_own, f32[2,1736,128]{2,1,0:T(8,128)S(1)} %get-tuple-element.81.ocean_own, f32[3456,384]{1,0:T(8,128)S(1)} %get-tuple-element.83.atmos_other, ...), custom_call_target="tpu_custom_call" | custom-call | bytes 6684672 | tf_op jit(solution)/shard_map/chunk/pallas_call | solution.py:34
  26.7 3.5 %collective-permute-start.9 = (bf16[8,272,384]{2,1,0:T(8,128)(2,1)S(1)}, bf16[8,272,384]{2,1,0:T(8,128)(2,1)S(1)}, u32[]{:S(2)}, u32[]{:S(2)}) collective-permute-start(bf16[8,272,384]{2,1,0:T(8,128)(2,1)S(1)} %get-tuple-element.86), channel_id=1, source_target_pairs={{0,1},{1,0},{2,3},{3,2},{4,5},{5,4},{6,7},{7,6},{8,9},{9,8},{10,11... | collective-permute-start | bytes 5013512 | tf_op jit(solution)/shard_map/ppermute | solution.py:560
  30.2 1.4 %input_grad.1 = (f32[256,384]{1,0:T(8,128)S(1)}, f32[4,256]{1,0:T(4,128)S(1)}) custom-call(bf16[256,384]{1,0:T(8,128)(2,1)S(1)} %get-tuple-element.69.stay_ref, bf16[256,384]{1,0:T(8,128)(2,1)S(1)} %get-tuple-element.70.give_ref, bf16[256,384]{1,0:T(8,128)(2,1)S(1)} %collective-permute-done.3.near_ref.near_any, ...), custom_call_target="tpu_custom_call" | custom-call | flops 2717908992 | bytes 2654208 | tf_op jit(solution)/shard_map/input_grad/pallas_call | solution.py:34
  31.6 1.8 %collective-permute-done.9 = bf16[8,272,384]{2,1,0:T(8,128)(2,1)S(1)} collective-permute-done((bf16[8,272,384]{2,1,0:T(8,128)(2,1)S(1)}, bf16[8,272,384]{2,1,0:T(8,128)(2,1)S(1)}, u32[]{:S(2)}, u32[]{:S(2)}) %collective-permute-start.9) | collective-permute-done | bytes 1671200 | tf_op jit(solution)/shard_map/ppermute | solution.py:560
  33.8 3.0 %collective-permute-start.10 = (bf16[4,1,96,384]{3,2,1,0:T(8,128)(2,1)S(1)}, bf16[4,1,96,384]{3,2,1,0:T(8,128)(2,1)S(1)}, u32[]{:S(2)}, u32[]{:S(2)}) collective-permute-start(bf16[4,1,96,384]{3,2,1,0:T(8,128)(2,1)S(1)} %get-tuple-element.88), channel_id=1, source_target_pairs={{0,2},{1,3},{2,0},{3,1},{4,6},{5,7},{6,4},{7,5},{8,10},{9,11},{10,... | collective-permute-start | bytes 884744 | tf_op jit(solution)/shard_map/ppermute | solution.py:560
  36.8 1.6 %collective-permute-start.13 = (bf16[2,2,96,384]{3,2,1,0:T(8,128)(2,1)S(1)}, bf16[2,2,96,384]{3,2,1,0:T(8,128)(2,1)S(1)}, u32[]{:S(2)}, u32[]{:S(2)}) collective-permute-start(bf16[2,2,96,384]{3,2,1,0:T(8,128)(2,1)S(1)} %get-tuple-element.96), channel_id=1, source_target_pairs={{0,4},{1,5},{2,6},{3,7},{4,0},{5,1},{6,2},{7,3},{8,12},{9,13},{10,... | collective-permute-start | bytes 884744 | tf_op jit(solution)/shard_map/ppermute | solution.py:560
  38.4 1.8 %collective-permute-start.5 = (f32[4,256]{1,0:T(4,128)S(1)}, f32[4,256]{1,0:T(4,128)S(1)}, u32[]{:S(2)}, u32[]{:S(2)}) collective-permute-start(f32[4,256]{1,0:T(4,128)S(1)} %get-tuple-element.76.done_ref), channel_id=1, source_target_pairs={{0,16},{16,0},{1,17},{17,1},{2,18},{18,2},{3,19},{19,3},{4,20},{20... | collective-permute-start | bytes 12296 | tf_op jit(solution)/shard_map/ppermute | solution.py:560
  40.2 1.4 %collective-permute-start.12 = (bf16[4,1,80,384]{3,2,1,0:T(8,128)(2,1)S(1)}, bf16[4,1,80,384]{3,2,1,0:T(8,128)(2,1)S(1)}, u32[]{:S(2)}, u32[]{:S(2)}) collective-permute-start(bf16[4,1,80,384]{3,2,1,0:T(8,128)(2,1)S(1)} %get-tuple-element.94), channel_id=1, source_target_pairs={{0,2},{1,3},{2,0},{3,1},{4,6},{5,7},{6,4},{7,5},{8,10},{9,11},{10,... | collective-permute-start | bytes 737288 | tf_op jit(solution)/shard_map/ppermute | solution.py:560
  41.5 1.7 %next.1 = (bf16[2,128,384]{2,1,0:T(8,128)(2,1)}, f32[8,128]{1,0:T(8,128)S(1)}) custom-call(bf16[256,384]{1,0:T(8,128)(2,1)S(1)} %get-tuple-element.69.stay_ref, bf16[256,384]{1,0:T(8,128)(2,1)S(1)} %get-tuple-element.70.give_ref, bf16[256,384]{1,0:T(8,128)(2,1)S(1)} %collective-permute-done.3.near_ref.near_any, ...), custom_call_target="tpu_custom_call" | custom-call | flops 2717908992 | bytes 2654208 | tf_op jit(solution)/shard_map/next/pallas_call | solution.py:34
  43.2 1.2 %last.1 = (bf16[2,128,384]{2,1,0:T(8,128)(2,1)}, f32[8,128]{1,0:T(8,128)S(1)}) custom-call(f32[256,384]{1,0:T(8,128)S(1)} %get-tuple-element.75.grad_ref, f32[4,256]{1,0:T(4,128)S(1)} %collective-permute-done.5.arrived_ref, f32[8,512]{1,0:T(8,128)S(1)} %get-tuple-element.64.wet_ref, f32[16,384]{1,0:T(8,128)S(1)} %fusion.9.terms_ref), custom_call_target="tpu_custom_call" | custom-call | tf_op jit(solution)/shard_map/last/pallas_call | solution.py:34
  44.6 3.4 %collective-permute-start.11 = (bf16[2,1,96,384]{3,2,0,1:T(8,128)(2,1)S(1)}, bf16[2,1,96,384]{3,2,0,1:T(8,128)(2,1)S(1)}, u32[]{:S(2)}, u32[]{:S(2)}) collective-permute-start(bf16[2,1,96,384]{3,2,0,1:T(8,128)(2,1)S(1)} %bitcast.53), channel_id=1, source_target_pairs={{0,4},{1,5},{2,6},{3,7},{4,0},{5,1},{6,2},{7,3},{8,12},{9,13},{10,... | collective-permute-start | bytes 442376 | tf_op jit(solution)/shard_map/ppermute | solution.py:560
  48.2 1.4 %collective-permute-start.15 = (bf16[1,2,96,384]{3,2,1,0:T(8,128)(2,1)S(1)}, bf16[1,2,96,384]{3,2,1,0:T(8,128)(2,1)S(1)}, u32[]{:S(2)}, u32[]{:S(2)}) collective-permute-start(bf16[1,2,96,384]{3,2,1,0:T(8,128)(2,1)S(1)} %get-tuple-element.103), channel_id=1, source_target_pairs={{0,8},{1,9},{2,10},{3,11},{4,12},{5,13},{6,14},{7,15},{8,0},{9,1},... | collective-permute-start | bytes 442376 | tf_op jit(solution)/shard_map/ppermute | solution.py:560
  49.7 2.9 %collective-permute-start.17 = (bf16[2,1,80,384]{3,2,0,1:T(8,128)(2,1)S(1)}, bf16[2,1,80,384]{3,2,0,1:T(8,128)(2,1)S(1)}, u32[]{:S(2)}, u32[]{:S(2)}) collective-permute-start(bf16[2,1,80,384]{3,2,0,1:T(8,128)(2,1)S(1)} %bitcast.54), channel_id=1, source_target_pairs={{0,4},{1,5},{2,6},{3,7},{4,0},{5,1},{6,2},{7,3},{8,12},{9,13},{10,... | collective-permute-start | bytes 368648 | tf_op jit(solution)/shard_map/ppermute | solution.py:560
  52.8 2.3 %collective-permute-start.14 = (bf16[1,1,96,384]{3,2,1,0:T(8,128)(2,1)S(1)}, bf16[1,1,96,384]{3,2,1,0:T(8,128)(2,1)S(1)}, u32[]{:S(2)}, u32[]{:S(2)}) collective-permute-start(bf16[1,1,96,384]{3,2,1,0:T(8,128)(2,1)S(1)} %get-tuple-element.101), channel_id=1, source_target_pairs={{0,8},{1,9},{2,10},{3,11},{4,12},{5,13},{6,14},{7,15},{8,0},{9,1},... | collective-permute-start | bytes 221192 | tf_op jit(solution)/shard_map/ppermute | solution.py:560
  55.1 0.9 %collective-permute-done.15 = bf16[1,2,96,384]{3,2,1,0:T(8,128)(2,1)S(1)} collective-permute-done((bf16[1,2,96,384]{3,2,1,0:T(8,128)(2,1)S(1)}, bf16[1,2,96,384]{3,2,1,0:T(8,128)(2,1)S(1)}, u32[]{:S(2)}, u32[]{:S(2)}) %collective-permute-start.15) | collective-permute-done | bytes 147488 | tf_op jit(solution)/shard_map/ppermute | solution.py:560
  56.0 0.9 %collective-permute-start.16 = (bf16[1,1,96,384]{3,2,1,0:T(8,128)(2,1)S(1)}, bf16[1,1,96,384]{3,2,1,0:T(8,128)(2,1)S(1)}, u32[]{:S(2)}, u32[]{:S(2)}) collective-permute-start(bf16[1,1,96,384]{3,2,1,0:T(8,128)(2,1)S(1)} %get-tuple-element.106), channel_id=1, source_target_pairs={{0,2},{1,3},{2,0},{3,1},{4,6},{5,7},{6,4},{7,5},{8,10},{9,11},{10,... | collective-permute-start | bytes 221192 | tf_op jit(solution)/shard_map/ppermute | solution.py:560
  56.9 1.7 %collective-permute-done.17 = bf16[2,1,80,384]{3,2,0,1:T(8,128)(2,1)S(1)} collective-permute-done((bf16[2,1,80,384]{3,2,0,1:T(8,128)(2,1)S(1)}, bf16[2,1,80,384]{3,2,0,1:T(8,128)(2,1)S(1)}, u32[]{:S(2)}, u32[]{:S(2)}) %collective-permute-start.17) | collective-permute-done | bytes 122912 | tf_op jit(solution)/shard_map/ppermute | solution.py:560
  59.2 1.4 %collective-permute-start.18 = (bf16[1,1,80,384]{3,2,1,0:T(8,128)(2,1)S(1)}, bf16[1,1,80,384]{3,2,1,0:T(8,128)(2,1)S(1)}, u32[]{:S(2)}, u32[]{:S(2)}) collective-permute-start(bf16[1,1,80,384]{3,2,1,0:T(8,128)(2,1)S(1)} %get-tuple-element.111), channel_id=1, source_target_pairs={{0,8},{1,9},{2,10},{3,11},{4,12},{5,13},{6,14},{7,15},{8,0},{9,1},... | collective-permute-start | bytes 184328 | tf_op jit(solution)/shard_map/ppermute | solution.py:560
  60.6 4.2 %collective-permute-done.18 = bf16[1,1,80,384]{3,2,1,0:T(8,128)(2,1)S(1)} collective-permute-done((bf16[1,1,80,384]{3,2,1,0:T(8,128)(2,1)S(1)}, bf16[1,1,80,384]{3,2,1,0:T(8,128)(2,1)S(1)}, u32[]{:S(2)}, u32[]{:S(2)}) %collective-permute-start.18) | collective-permute-done | bytes 61472 | tf_op jit(solution)/shard_map/ppermute | solution.py:560
  64.8 0.8 %finish.1 = (f32[648,128]{1,0:T(8,128)}, f32[162,128]{1,0:T(8,128)}) custom-call(bf16[96,384]{1,0:T(8,128)(2,1)S(1)} %bitcast.47, bf16[96,384]{1,0:T(8,128)(2,1)S(1)} %bitcast.48, bf16[96,384]{1,0:T(8,128)(2,1)S(1)} %bitcast.49, bf16[96,384]{1,0:T(8,128)(2,1)S(1)} %bitcast.50, bf16[80,384]{1,0:T(8,128)(2,1)S(1)} %bitcast.51, bf16[80,384]{1,0:T(8,128)(2,1)S(1)} %bitcast.52), custom_call_target="tpu_custom_call" | custom-call | tf_op jit(solution)/shard_map/finish/pallas_call | solution.py:34
  (39 shorter events, 5.3 us)
Async XLA Ops:
  2.7 7.1 %collective-permute-start = (bf16[272,384]{1,0:T(8,128)(2,1)}, bf16[272,384]{1,0:T(8,128)(2,1)S(1)}, u32[]{:S(2)}, u32[]{:S(2)}) collective-permute-start(bf16[272,384]{1,0:T(8,128)(2,1)} %get-tuple-element.61), channel_id=1, source_target_pairs={{0,1},{1,0},{2,3},{3,2},{4,5},{5,4},{6,7},{7,6},{8,9},{9,8},{10,11... | collective-permute-start | bytes 626696 | tf_op jit(solution)/shard_map/ppermute | solution.py:560
  3.2 6.5 %collective-permute-start.1 = (bf16[272,384]{1,0:T(8,128)(2,1)}, bf16[272,384]{1,0:T(8,128)(2,1)S(1)}, u32[]{:S(2)}, u32[]{:S(2)}) collective-permute-start(bf16[272,384]{1,0:T(8,128)(2,1)} %get-tuple-element.62), channel_id=1, source_target_pairs={{1,2},{2,1},{3,4},{4,3},{5,6},{6,5},{7,8},{8,7},{9,10},{10,9},{11,... | collective-permute-start | bytes 626696 | tf_op jit(solution)/shard_map/ppermute | solution.py:566
  3.9 17.2 %collective-permute-start.6 = (bf16[256,384]{1,0:T(8,128)(2,1)}, bf16[256,384]{1,0:T(8,128)(2,1)S(1)}, u32[]{:S(2)}, u32[]{:S(2)}) collective-permute-start(bf16[256,384]{1,0:T(8,128)(2,1)} %get-tuple-element.78), channel_id=1, source_target_pairs={{0,16},{16,0},{1,17},{17,1},{2,18},{18,2},{3,19},{19,3},{4,20},{20... | collective-permute-start | bytes 589832 | tf_op jit(solution)/shard_map/ppermute | solution.py:560
  6.4 1.5 %copy-start = (bf16[2,3,3,192,192]{4,3,2,1,0:T(8,128)(2,1)S(1)}, bf16[2,3,3,192,192]{4,3,2,1,0:T(8,128)(2,1)}, u32[]{:S(2)}) copy-start(bf16[2,3,3,192,192]{4,3,2,1,0:T(8,128)(2,1)} %param.12) | copy-start | bytes 3981316
  7.9 1.0 %copy-start.1 = (bf16[528,384]{1,0:T(8,128)(2,1)S(1)}, bf16[528,384]{1,0:T(8,128)(2,1)}, u32[]{:S(2)}) copy-start(bf16[528,384]{1,0:T(8,128)(2,1)} %get-tuple-element.59.own_in) | copy-start | bytes 1216516
  8.9 0.7 %copy-start.2 = (bf16[4,384]{1,0:T(4,128)(2,1)S(1)}, bf16[4,384]{1,0:T(4,128)(2,1)}, u32[]{:S(2)}) copy-start(bf16[4,384]{1,0:T(4,128)(2,1)} %coupling_ref.1) | copy-start | bytes 9220
  8.9 0.7 %copy-start.3 = (bf16[384,4]{0,1:T(4,128)(2,1)S(1)}, bf16[384,4]{0,1:T(4,128)(2,1)}, u32[]{:S(2)}) copy-start(bf16[384,4]{0,1:T(4,128)(2,1)} %param.16) | copy-start | bytes 9220
  8.9 0.7 %copy-start.4 = (bf16[4,192]{1,0:T(4,128)(2,1)S(1)}, bf16[4,192]{1,0:T(4,128)(2,1)}, u32[]{:S(2)}) copy-start(bf16[4,192]{1,0:T(4,128)(2,1)} %param.15) | copy-start | bytes 4612
  8.9 0.7 %copy-start.5 = (bf16[192,4]{0,1:T(4,128)(2,1)S(1)}, bf16[192,4]{0,1:T(4,128)(2,1)}, u32[]{:S(2)}) copy-start(bf16[192,4]{0,1:T(4,128)(2,1)} %param.14) | copy-start | bytes 4612
  10.0 3.7 %collective-permute-start.2 = (f32[4,512]{1,0:T(4,128)S(1)}, f32[4,512]{1,0:T(4,128)S(1)}, u32[]{:S(2)}, u32[]{:S(2)}) collective-permute-start(f32[4,512]{1,0:T(4,128)S(1)} %get-tuple-element.65.sent_ref), channel_id=1, source_target_pairs={{0,16},{16,0},{1,17},{17,1},{2,18},{18,2},{3,19},{19,3},{4,20},{20... | collective-permute-start | bytes 24584 | tf_op jit(solution)/shard_map/ppermute | solution.py:560
  12.0 9.1 %collective-permute-start.7 = (bf16[256,384]{1,0:T(8,128)(2,1)S(1)}, bf16[256,384]{1,0:T(8,128)(2,1)S(1)}, u32[]{:S(2)}, u32[]{:S(2)}) collective-permute-start(bf16[256,384]{1,0:T(8,128)(2,1)S(1)} %get-tuple-element.79), channel_id=1, source_target_pairs={{0,16},{16,0},{1,17},{17,1},{2,18},{18,2},{3,19},{19,3},{4,20},{20... | collective-permute-start | bytes 589832 | tf_op jit(solution)/shard_map/ppermute | solution.py:560
  15.9 10.0 %collective-permute-start.3 = (bf16[256,384]{1,0:T(8,128)(2,1)S(1)}, bf16[256,384]{1,0:T(8,128)(2,1)S(1)}, u32[]{:S(2)}, u32[]{:S(2)}) collective-permute-start(bf16[256,384]{1,0:T(8,128)(2,1)S(1)} %get-tuple-element.71), channel_id=1, source_target_pairs={{0,1},{1,0},{2,3},{3,2},{4,5},{5,4},{6,7},{7,6},{8,9},{9,8},{10,11... | collective-permute-start | bytes 589832 | tf_op jit(solution)/shard_map/ppermute | solution.py:560
  18.4 7.5 %collective-permute-start.4 = (bf16[256,384]{1,0:T(8,128)(2,1)S(1)}, bf16[256,384]{1,0:T(8,128)(2,1)S(1)}, u32[]{:S(2)}, u32[]{:S(2)}) collective-permute-start(bf16[256,384]{1,0:T(8,128)(2,1)S(1)} %get-tuple-element.72), channel_id=1, source_target_pairs={{1,2},{2,1},{3,4},{4,3},{5,6},{6,5},{7,8},{8,7},{9,10},{10,9},{11,... | collective-permute-start | bytes 589832 | tf_op jit(solution)/shard_map/ppermute | solution.py:566
  19.1 5.7 %collective-permute-start.8 = (bf16[256,384]{1,0:T(8,128)(2,1)S(1)}, bf16[256,384]{1,0:T(8,128)(2,1)S(1)}, u32[]{:S(2)}, u32[]{:S(2)}) collective-permute-start(bf16[256,384]{1,0:T(8,128)(2,1)S(1)} %get-tuple-element.70.give_ref), channel_id=1, source_target_pairs={{0,16},{16,0},{1,17},{17,1},{2,18},{18,2},{3,19},{19,3},{4,20},{20... | collective-permute-start | bytes 589832 | tf_op jit(solution)/shard_map/ppermute | solution.py:560
  26.7 6.7 %collective-permute-start.9 = (bf16[8,272,384]{2,1,0:T(8,128)(2,1)S(1)}, bf16[8,272,384]{2,1,0:T(8,128)(2,1)S(1)}, u32[]{:S(2)}, u32[]{:S(2)}) collective-permute-start(bf16[8,272,384]{2,1,0:T(8,128)(2,1)S(1)} %get-tuple-element.86), channel_id=1, source_target_pairs={{0,1},{1,0},{2,3},{3,2},{4,5},{5,4},{6,7},{7,6},{8,9},{9,8},{10,11... | collective-permute-start | bytes 5013512 | tf_op jit(solution)/shard_map/ppermute | solution.py:560
  33.8 10.8 %collective-permute-start.10 = (bf16[4,1,96,384]{3,2,1,0:T(8,128)(2,1)S(1)}, bf16[4,1,96,384]{3,2,1,0:T(8,128)(2,1)S(1)}, u32[]{:S(2)}, u32[]{:S(2)}) collective-permute-start(bf16[4,1,96,384]{3,2,1,0:T(8,128)(2,1)S(1)} %get-tuple-element.88), channel_id=1, source_target_pairs={{0,2},{1,3},{2,0},{3,1},{4,6},{5,7},{6,4},{7,5},{8,10},{9,11},{10,... | collective-permute-start | bytes 884744 | tf_op jit(solution)/shard_map/ppermute | solution.py:560
  36.8 11.3 %collective-permute-start.13 = (bf16[2,2,96,384]{3,2,1,0:T(8,128)(2,1)S(1)}, bf16[2,2,96,384]{3,2,1,0:T(8,128)(2,1)S(1)}, u32[]{:S(2)}, u32[]{:S(2)}) collective-permute-start(bf16[2,2,96,384]{3,2,1,0:T(8,128)(2,1)S(1)} %get-tuple-element.96), channel_id=1, source_target_pairs={{0,4},{1,5},{2,6},{3,7},{4,0},{5,1},{6,2},{7,3},{8,12},{9,13},{10,... | collective-permute-start | bytes 884744 | tf_op jit(solution)/shard_map/ppermute | solution.py:560
  38.4 4.9 %collective-permute-start.5 = (f32[4,256]{1,0:T(4,128)S(1)}, f32[4,256]{1,0:T(4,128)S(1)}, u32[]{:S(2)}, u32[]{:S(2)}) collective-permute-start(f32[4,256]{1,0:T(4,128)S(1)} %get-tuple-element.76.done_ref), channel_id=1, source_target_pairs={{0,16},{16,0},{1,17},{17,1},{2,18},{18,2},{3,19},{19,3},{4,20},{20... | collective-permute-start | bytes 12296 | tf_op jit(solution)/shard_map/ppermute | solution.py:560
  40.2 9.4 %collective-permute-start.12 = (bf16[4,1,80,384]{3,2,1,0:T(8,128)(2,1)S(1)}, bf16[4,1,80,384]{3,2,1,0:T(8,128)(2,1)S(1)}, u32[]{:S(2)}, u32[]{:S(2)}) collective-permute-start(bf16[4,1,80,384]{3,2,1,0:T(8,128)(2,1)S(1)} %get-tuple-element.94), channel_id=1, source_target_pairs={{0,2},{1,3},{2,0},{3,1},{4,6},{5,7},{6,4},{7,5},{8,10},{9,11},{10,... | collective-permute-start | bytes 737288 | tf_op jit(solution)/shard_map/ppermute | solution.py:560
  44.6 8.1 %collective-permute-start.11 = (bf16[2,1,96,384]{3,2,0,1:T(8,128)(2,1)S(1)}, bf16[2,1,96,384]{3,2,0,1:T(8,128)(2,1)S(1)}, u32[]{:S(2)}, u32[]{:S(2)}) collective-permute-start(bf16[2,1,96,384]{3,2,0,1:T(8,128)(2,1)S(1)} %bitcast.53), channel_id=1, source_target_pairs={{0,4},{1,5},{2,6},{3,7},{4,0},{5,1},{6,2},{7,3},{8,12},{9,13},{10,... | collective-permute-start | bytes 442376 | tf_op jit(solution)/shard_map/ppermute | solution.py:560
  48.2 7.8 %collective-permute-start.15 = (bf16[1,2,96,384]{3,2,1,0:T(8,128)(2,1)S(1)}, bf16[1,2,96,384]{3,2,1,0:T(8,128)(2,1)S(1)}, u32[]{:S(2)}, u32[]{:S(2)}) collective-permute-start(bf16[1,2,96,384]{3,2,1,0:T(8,128)(2,1)S(1)} %get-tuple-element.103), channel_id=1, source_target_pairs={{0,8},{1,9},{2,10},{3,11},{4,12},{5,13},{6,14},{7,15},{8,0},{9,1},... | collective-permute-start | bytes 442376 | tf_op jit(solution)/shard_map/ppermute | solution.py:560
  49.7 8.9 %collective-permute-start.17 = (bf16[2,1,80,384]{3,2,0,1:T(8,128)(2,1)S(1)}, bf16[2,1,80,384]{3,2,0,1:T(8,128)(2,1)S(1)}, u32[]{:S(2)}, u32[]{:S(2)}) collective-permute-start(bf16[2,1,80,384]{3,2,0,1:T(8,128)(2,1)S(1)} %bitcast.54), channel_id=1, source_target_pairs={{0,4},{1,5},{2,6},{3,7},{4,0},{5,1},{6,2},{7,3},{8,12},{9,13},{10,... | collective-permute-start | bytes 368648 | tf_op jit(solution)/shard_map/ppermute | solution.py:560
  52.8 12.0 %collective-permute-start.14 = (bf16[1,1,96,384]{3,2,1,0:T(8,128)(2,1)S(1)}, bf16[1,1,96,384]{3,2,1,0:T(8,128)(2,1)S(1)}, u32[]{:S(2)}, u32[]{:S(2)}) collective-permute-start(bf16[1,1,96,384]{3,2,1,0:T(8,128)(2,1)S(1)} %get-tuple-element.101), channel_id=1, source_target_pairs={{0,8},{1,9},{2,10},{3,11},{4,12},{5,13},{6,14},{7,15},{8,0},{9,1},... | collective-permute-start | bytes 221192 | tf_op jit(solution)/shard_map/ppermute | solution.py:560
  56.0 8.8 %collective-permute-start.16 = (bf16[1,1,96,384]{3,2,1,0:T(8,128)(2,1)S(1)}, bf16[1,1,96,384]{3,2,1,0:T(8,128)(2,1)S(1)}, u32[]{:S(2)}, u32[]{:S(2)}) collective-permute-start(bf16[1,1,96,384]{3,2,1,0:T(8,128)(2,1)S(1)} %get-tuple-element.106), channel_id=1, source_target_pairs={{0,2},{1,3},{2,0},{3,1},{4,6},{5,7},{6,4},{7,5},{8,10},{9,11},{10,... | collective-permute-start | bytes 221192 | tf_op jit(solution)/shard_map/ppermute | solution.py:560
  59.2 5.6 %collective-permute-start.18 = (bf16[1,1,80,384]{3,2,1,0:T(8,128)(2,1)S(1)}, bf16[1,1,80,384]{3,2,1,0:T(8,128)(2,1)S(1)}, u32[]{:S(2)}, u32[]{:S(2)}) collective-permute-start(bf16[1,1,80,384]{3,2,1,0:T(8,128)(2,1)S(1)} %get-tuple-element.111), channel_id=1, source_target_pairs={{0,8},{1,9},{2,10},{3,11},{4,12},{5,13},{6,14},{7,15},{8,0},{9,1},... | collective-permute-start | bytes 184328 | tf_op jit(solution)/shard_map/ppermute | solution.py:560
where the time goes:
time: 65.8 us; the launch traced here: 65.6 us
  starting transfers between devices  34.7 us (53%)
  Pallas kernels  16.1 us (24%)
  waiting for transfers between devices  10.9 us (17%)
  local copies, waits for them, and re-layouts  2.97 us (5%)
  between operations  0.78 us (1%)
    ppermute x17, starting transfers between devices, swapped(): return lax.ppermute(value, axis, pairs)  33.4 us
    pallas_call x19, Pallas kernels, call(): pl.pallas_call(kernel, out_shape=outs, in_specs=in_specs or [WHOLE] * len...  16.1 us
    ppermute x17, waiting for transfers between devices, swapped(): return lax.ppermute(value, axis, pairs)  10.9 us
    unnamed x12, local copies, waits for them, and re-layouts  2.96 us
    ppermute x2, starting transfers between devices, halo(): far = lax.ppermute(far, 'lat', pairs)  1.32 us
  transfers between devices with their start and end apart: 19, of which 8 were waited for; matrix products, arithmetic and copies ran while one was open for 0% of the time, Pallas kernels for 18%

commit v1 on v0

--- a/solution.py
+++ b/solution.py
@@ -338,6 +338,15 @@
     return store
 
 
+def near_rows(near_ref, part, cols):
+    if len(near_ref.shape) == 2:
+        return near_ref[part * cols : (part + 1) * cols, :]
+    count, tall = near_ref.shape[0] // 2, near_ref.shape[1]
+    taken = cols // count
+    pieces = [near_ref[index, tall - taken :, :] for index in range(part * count, (part + 1) * count)]
+    return jnp.concatenate(pieces, axis=0)
+
+
 def hidden_and_grad(stay_ref, give_ref):
     stay, give = stay_ref[...], give_ref[...]
     return jnp.where(on_ocean(), give, stay), jnp.where(on_ocean(), stay, give)
@@ -384,74 +393,83 @@
         grad_ocean(whole_pad(early_ref, edge_ref, cols), late, False, cols, store_into(ocean_out))
 
 
-def chunk_rows(keep_ref, send_ref, atmos_all, ocean_all, chunks):
-    channels = keep_ref.shape[2]
+def chunk_rows(out_ref, side, tall, atmos_all, ocean_all, chunks):
+    channels = out_ref.shape[2]
     pieces = ocean_all.shape[0]
     atmos_rows = atmos_all.shape[0] // chunks
     ocean_rows = atmos_rows // 2
-    taken = keep_ref.shape[1] - atmos_rows
-    core = lax.rem(lax.axis_index("lat"), 2)
+    taken = tall - atmos_rows
     blank = jnp.zeros((taken, channels - 128 * pieces), F32)
-    for out_ref, side in ((send_ref, 1 - core), (keep_ref, core)):
+    for pair in range(chunks // 2):
+        start = pl.multiple_of(atmos_rows * (2 * pair + side), 8)
+        upper = atmos_all[pl.ds(start, atmos_rows), :]
+        start = ocean_rows * (2 * pair + side)
+        halves = []
+        for odd in range(2):
+            parts = [ocean_all.at[piece][pl.ds(start + odd, taken, 2), :] for piece in range(pieces)]
+            halves.append(jnp.concatenate(parts + [blank], axis=1))
+        lower = halves[0] + pltpu.roll(halves[1], channels // 2, 1)
+        out_ref[pair, 0:tall, :] = jnp.concatenate([upper, lower], axis=0).astype(BF16)
+
+
+def chunk_kernel(atmos_own, ocean_own, atmos_other, ocean_other, *refs, chunks, tall, sent):
+    out_ref = refs[-1]
+    core = own_bit(0)
+    side = 1 - core if sent else core
+    if sent:
+        near_ref = refs[0]
+        taken = out_ref.shape[1] - tall
         for pair in range(chunks // 2):
-            start = pl.multiple_of(atmos_rows * (2 * pair + side), 8)
-            upper = atmos_all[pl.ds(start, atmos_rows), :]
-            start = ocean_rows * (2 * pair + side)
-            halves = []
-            for odd in range(2):
-                parts = [ocean_all.at[piece][pl.ds(start + odd, taken, 2), :] for piece in range(pieces)]
-                halves.append(jnp.concatenate(parts + [blank], axis=1))
-            lower = halves[0] + pltpu.roll(halves[1], channels // 2, 1)
-            out_ref[pair] = jnp.concatenate([upper, lower], axis=0).astype(BF16)
-
-
-def chunk_kernel(
-    atmos_own, ocean_own, atmos_other, ocean_other, near_any, far_any, keep_ref, send_ref, *, chunks
-):
+            out_ref[pair, tall:, :] = near_ref[pair * taken : (pair + 1) * taken, :]
+
     @pl.when(on_ocean())
     def _():
-        chunk_rows(keep_ref, send_ref, atmos_other, ocean_own, chunks)
+        chunk_rows(out_ref, side, tall, atmos_other, ocean_own, chunks)
 
     @pl.when(jnp.logical_not(on_ocean()))
     def _():
-        chunk_rows(keep_ref, send_ref, atmos_own, ocean_other, chunks)
-
-
-def halve(keep_ref, came_ref, keep_out, send_out, bit, rows):
-    own = own_bit(bit)
-    for out_ref, side in ((send_out, 1 - own), (keep_out, own)):
-        for outer in range(keep_ref.shape[0]):
-            for inner in range(keep_ref.shape[2]):
-                total = keep_ref[outer, side, inner, rows, :].astype(F32)
-                total = total + came_ref[outer, side, inner, rows, :].astype(F32)
-                out_ref[outer, inner] = total.astype(BF16)
-
-
-def split_kernel(keep_ref, came_ref, done_ref, *outs, cuts):
-    by_z = [ref.reshape(2, 2, 2, *keep_ref.shape[3:]) for ref in (keep_ref, came_ref)]
+        chunk_rows(out_ref, side, tall, atmos_own, ocean_other, chunks)
+
+
+def halve(keep_ref, came_ref, out_ref, side, rows):
+    for outer in range(keep_ref.shape[0]):
+        for inner in range(keep_ref.shape[2]):
+            total = keep_ref[outer, side, inner, rows, :].astype(F32)
+            total = total + came_ref[outer, side, inner, rows, :].astype(F32)
+            out_ref[outer, inner] = total.astype(BF16)
+
+
+def split_kernel(keep_ref, came_ref, *refs, cuts, sent):
+    by_z = [ref.reshape(2, 2, 2, *ref.shape[3:]) for ref in (keep_ref, came_ref)]
     start = 0
     for index, rows in enumerate(cuts):
-        refs, bit = (by_z, 2) if index == 1 else ((keep_ref, came_ref), 1)
-        halve(*refs, *outs[2 * index : 2 * index + 2], bit, slice(start, start + rows))
+        pair, bit = (by_z, 2) if index == 1 else ((keep_ref, came_ref), 1)
+        own = own_bit(bit)
+        halve(*pair, refs[index], 1 - own if sent else own, slice(start, start + rows))
         start += rows
-
-
-def halve_kernel(keep_ref, came_ref, *refs, bit):
-    keep_out, send_out, mark_ref = refs[-3:]
-    halve(keep_ref, came_ref, keep_out, send_out, bit, slice(None))
-    mark_ref[...] = jnp.zeros_like(mark_ref)
+    if sent:
+        refs[-1][...] = jnp.zeros_like(refs[-1])
+
+
+def halve_kernel(keep_ref, came_ref, *refs, bit, marked):
+    outs = refs[-3:] if marked else refs[-2:]
+    own = own_bit(bit)
+    halve(keep_ref, came_ref, outs[1], 1 - own, slice(None))
+    halve(keep_ref, came_ref, outs[0], own, slice(None))
+    if marked:
+        outs[2][...] = jnp.zeros_like(outs[2])
 
 
 MARK = shape((8, 128), F32)
 
 
-def halved(keep, came, bit, dims, after):
+def halved(keep, came, bit, dims, after, marked=True):
     outer, inner, rows, channels = dims[0], dims[1], keep.shape[-2], keep.shape[-1]
     keep, came = (part.reshape(outer, 2, inner, rows, channels) for part in (keep, came))
     out = shape((outer, inner, rows, channels), BF16)
     return call(
-        functools.partial(halve_kernel, bit=bit),
-        [out, out, MARK],
+        functools.partial(halve_kernel, bit=bit, marked=marked),
+        [out, out] + [MARK] * marked,
         [keep, came, *after],
         [WHOLE] * 2 + [ANYWHERE] * len(after),
         moved=8 * outer * inner * rows * channels,
@@ -459,37 +477,45 @@
     )
 
 
-def scatter_sum(keep, came, done_before, done_next):
+def split(keep, came):
     pairs, tall, channels = keep.shape
     cuts = [16 * (tall // 16 * part // 17) for part in (6, 6)]
     cuts.append(tall - sum(cuts))
-    outs = []
-    for index, rows in enumerate(cuts):
-        outs += [shape(((2, 2) if index == 1 else (4, 1)) + (rows, channels), BF16)] * 2
-    keep, came = (part.reshape(4, 2, 1, tall, channels) for part in (keep, came))
-    parts = call(
-        functools.partial(split_kernel, cuts=cuts),
-        outs,
-        [keep, came, done_before],
-        [WHOLE] * 2 + [ANYWHERE],
-        moved=6 * pairs * tall * channels,
-        name="split",
-    )
-    a_keep, a_send, b_keep, b_send, c_keep, c_send = parts
+    outs = [
+        shape(((2, 2) if index == 1 else (4, 1)) + (rows, channels), BF16) for index, rows in enumerate(cuts)
+    ]
+    inputs = [part.reshape(4, 2, 1, *part.shape[1:]) for part in (keep, came)]
+    kept, sent = (
+        call(
+            functools.partial(split_kernel, cuts=cuts, sent=is_sent),
+            outs + [MARK] * is_sent,
+            inputs,
+            moved=3 * pairs * tall * channels,
+            name="split",
+        )
+        for is_sent in (False, True)
+    )
+    return kept, sent[:3], sent[3]
+
+
+def scatter_sum(kept, sent, before_b, finish_last):
+    (a_keep, b_keep, c_keep), (a_send, b_send, c_send) = kept, sent
+    channels = a_keep.shape[-1]
     a_came = swapped(a_send, "lat", 2)
     b_came = swapped(b_send, "lat", 4)
     c_came = swapped(c_send, "lat", 2)
-    a_keep, a_send, mark = halved(a_keep, a_came, 2, (2, 1), done_next)
+    b_keep, b_send, mark = halved(b_keep, b_came, 3, (1, 2), before_b)
+    b_came = swapped(b_send, "lat", 8)
+    mark = finish_last(mark)
+    a_keep, a_send, mark = halved(a_keep, a_came, 2, (2, 1), [mark])
     a_came = swapped(a_send, "lat", 4)
-    b_keep, b_send, mark = halved(b_keep, b_came, 3, (1, 2), [mark])
-    b_came = swapped(b_send, "lat", 8)
     c_keep, c_send, mark = halved(c_keep, c_came, 2, (2, 1), [mark])
     c_came = swapped(c_send, "lat", 4)
+    b_keep, b_send, mark = halved(b_keep, b_came, 1, (1, 1), [mark])
+    b_came = swapped(b_send, "lat", 2)
     a_keep, a_send, mark = halved(a_keep, a_came, 3, (1, 1), [mark])
     a_came = swapped(a_send, "lat", 8)
-    b_keep, b_send, mark = halved(b_keep, b_came, 1, (1, 1), [mark])
-    b_came = swapped(b_send, "lat", 2)
-    c_keep, c_send, mark = halved(c_keep, c_came, 3, (1, 1), [mark])
+    c_keep, c_send = halved(c_keep, c_came, 3, (1, 1), [mark], False)
     c_came = swapped(c_send, "lat", 8)
     return [part.reshape(-1, channels) for part in (a_keep, a_came, b_keep, b_came, c_keep, c_came)]
 
@@ -514,11 +540,11 @@
 
 
 def input_grad_kernel(
-    stay_ref, give_ref, near_ref, far_ref, gpad_ref, wet_ref, terms_ref, atmos_ref, ocean_ref,
-    grad_ref, sent_ref, *, cols,
+    stay_ref, give_ref, near_ref, far_ref, gpad_ref, wet_ref, terms_ref, atmos_ref, ocean_ref, *refs, cols
 ):
+    grad_ref, sent_ref = refs[-2:]
     middle = hidden_and_grad(stay_ref, give_ref)[1]
-    low, high = low_and_high(near_ref[cols:, :], far_ref[cols:, :])
+    low, high = low_and_high(near_rows(near_ref, 1, cols), far_ref[cols:, :])
     pad = jnp.concatenate([low, middle, high], axis=0)
     own = slice(cols, 3 * cols)
     convolve(pad, grad_ref, atmos_ref, ocean_ref, 0, True, cols)
@@ -534,7 +560,7 @@
     next_ref, mark_ref, second_ref, *, cols,
 ):
     middle = hidden_and_grad(stay_ref, give_ref)[0]
-    low, high = low_and_high(near_ref[0:cols, :], far_ref[0:cols, :])
+    low, high = low_and_high(near_rows(near_ref, 0, cols), far_ref[0:cols, :])
     pad = jnp.concatenate([low, middle, high], axis=0)
     own = slice(cols, 3 * cols)
     convolve(pad, second_ref, atmos_ref, ocean_ref, 1, False, cols)
@@ -544,7 +570,8 @@
     mark_ref[...] = jnp.zeros_like(mark_ref)
 
 
-def last_kernel(grad_ref, arrived_ref, wet_ref, terms_ref, out_ref, mark_ref, *, cols):
+def last_kernel(grad_ref, arrived_ref, wet_ref, terms_ref, *refs, cols):
+    out_ref, mark_ref = refs[-2:]
     own = slice(cols, 3 * cols)
     wet = wet_ref[0:1, own], wet_ref[1:2, own]
     arrived = jnp.where(on_ocean(), arrived_ref[...] * wet_ref[2:3, own], arrived_ref[...])
@@ -560,11 +587,9 @@
     return lax.ppermute(value, axis, pairs)
 
 
-def halo(near, far):
-    count = lax.axis_size("lat")
-    pairs = [(i, i + 1 if i % 2 else i - 1) for i in range(1, count - 1)]
-    far = lax.ppermute(far, "lat", pairs)
-    return swapped(near, "lat", 1), far
+def far_halo(far):
+    pairs = [(i, i + 1 if i % 2 else i - 1) for i in range(1, lax.axis_size("lat") - 1)]
+    return lax.ppermute(far, "lat", pairs)
 
 
 def local(
@@ -620,7 +645,7 @@
         name="pack",
         limit=PACK_VMEM,
     )
-    near, far = halo(near, far)
+    near, far = swapped(near, "lat", 1), far_halo(far)
     other_early = swapped(own_early, "grp", 1)
     wide = -(-narrow // 128) * 128
     own, atmos_flat, ocean_flat = call(
@@ -665,7 +690,7 @@
     )
     late = swapped(give, "grp", 1)
 
-    near, far = halo(near, far)
+    far = far_halo(far)
 
     atmos_rows = 9 * channels // count
     ocean_rows = 9 * narrow // count
@@ -689,21 +714,31 @@
         name="other_grads",
     )
     if chunked:
-        part = shape((count // 2, tall, channels), BF16)
-        keep, send = call(
-            bound(chunk_kernel, chunks=count),
-            [part, part],
-            [atmos_sum, ocean_sum, atmos_other, ocean_other, near, far],
-            [WHOLE] * 4 + [ANYWHERE] * 2,
-            moved=4 * count * tall * channels,
-            name="chunk",
+        taken = 2 * cols // (count // 2)
+        sums = [atmos_sum, ocean_sum, atmos_other, ocean_other]
+        send, keep = (
+            call(
+                bound(chunk_kernel, chunks=count, tall=tall, sent=sent),
+                shape((count // 2, tall + taken * sent, channels), BF16),
+                sums + [near, far] * sent,
+                [WHOLE] * (4 + sent) + [ANYWHERE] * sent,
+                moved=2 * count * tall * channels,
+                name="chunk",
+            )
+            for sent in (True, False)
         )
-        came = swapped(send, "lat", 1)
+        near = swapped(send, "lat", 1)
+        kept, parts, split_mark = split(keep, near)
+        after_split = [split_mark]
+    else:
+        near = swapped(near, "lat", 1)
+        after_split = []
 
     grad, sent_back = call(
         bound(input_grad_kernel, cols=cols),
         [shape((cells, channels), F32), shape((4, cells), F32)],
-        [stay, give, near, far, gpad, wet, terms, atmos_flat, ocean_flat],
+        [stay, give, near, far, gpad, wet, terms, atmos_flat, ocean_flat, *after_split],
+        [WHOLE] * 9 + [ANYWHERE] * len(after_split),
         **conv_cost,
         name="input_grad",
     )
@@ -717,25 +752,37 @@
         **conv_cost,
         name="next",
     )
-    field_grad, last_mark = call(
-        bound(last_kernel, cols=cols),
-        [shape(x.shape, BF16), MARK],
-        [grad, returned, wet, terms],
-        name="last",
-    )
+
+    def field_grads(*after):
+        return call(
+            bound(last_kernel, cols=cols),
+            [shape(x.shape, BF16), MARK],
+            [grad, returned, wet, terms, *after],
+            [WHOLE] * 4 + [ANYWHERE] * len(after),
+            name="last",
+        )
 
     if chunked:
+        made = []
+
+        def finish_last(mark):
+            made.extend(field_grads(mark))
+            return made[1]
+
+        sums = scatter_sum(kept, parts, [returned, next_mark], finish_last)
+        field_grad = made[0]
         atmos_chunk, ocean_chunk = call(
             bound(finish_kernel, atmos_factor=atmos_factor, ocean_factor=ocean_factor),
             [
                 shape((atmos_rows * channels // 128, 128), F32),
                 shape((ocean_rows * narrow // 128, 128), F32),
             ],
-            scatter_sum(keep, came, sent_back, [next_mark, last_mark]),
+            sums,
             name="finish",
         )
         atmos_total, ocean_total = atmos_chunk.reshape(-1), ocean_chunk.reshape(-1)
     else:
+        field_grad = field_grads()[0]
         atmos_all = jnp.where(is_ocean, atmos_other, atmos_sum)
         ocean_all = jnp.where(is_ocean, ocean_sum, ocean_other)
         atmos_total = atmos_factor * lax.psum_scatter(

time: 65.8 us -> 65.2 us (level)
  starting transfers between devices: 34.7 us -> 30.3 us
  waiting for transfers between devices: 10.9 us -> 15.1 us
    ppermute x17 -> x16, starting transfers between devices: 33.4 us -> 29 us  [swapped(): return lax.ppermute(value, axis, pairs)]
    ppermute x17 -> x16, waiting for transfers between devices: 10.9 us -> 15.1 us  [swapped(): return lax.ppermute(value, axis, pairs)]
    pallas_call x19 -> x21, Pallas kernels: 16.1 us -> 15.7 us  [call(): pl.pallas_call(kernel, out_shape=outs, in_specs=in_specs or [WHOLE] * len...]
  transfers between devices with their start and end apart: 19 -> 18, of which waited for: 8 -> 8; matrix products, arithmetic and copies ran while one was open for 0% -> 0% of each run, Pallas kernels for 18% -> 19%
where the time goes in v1:
time: 65.2 us; the launch traced here: 64.9 us
  starting transfers between devices  30.3 us (46%)
  Pallas kernels  15.7 us (24%)
  waiting for transfers between devices  15.1 us (23%)
  local copies, waits for them, and re-layouts  2.97 us (5%)
  between operations  0.8 us (1%)
    ppermute x16, starting transfers between devices, swapped(): return lax.ppermute(value, axis, pairs)  29 us
    pallas_call x21, Pallas kernels, call(): pl.pallas_call(kernel, out_shape=outs, in_specs=in_specs or [WHOLE] * len...  15.7 us
    ppermute x16, waiting for transfers between devices, swapped(): return lax.ppermute(value, axis, pairs)  15.1 us
    unnamed x12, local copies, waits for them, and re-layouts  2.96 us
    ppermute x2, starting transfers between devices, far_halo(): return lax.ppermute(far, 'lat', pairs)  1.34 us
  transfers between devices with their start and end apart: 18, of which 8 were waited for; matrix products, arithmetic and copies ran while one was open for 0% of the time, Pallas kernels for 19%

profile of v1, /device:TPU:0, one launch (start us, length us, event | category | flops | bytes accessed | tf_op | source)
XLA Modules:
  0.0 64.9 jit_solution(4850301968076950662)
XLA Ops:
  0.6 2.0 %pack.1 = (bf16[272,384]{1,0:T(8,128)(2,1)}, bf16[272,384]{1,0:T(8,128)(2,1)}, bf16[256,384]{1,0:T(8,128)(2,1)}, bf16[528,384]{1,0:T(8,128)(2,1)}) custom-call(bf16[2,128,384]{2,1,0:T(8,128)(2,1)} %bitcast.58, bf16[2,128,384]{2,1,0:T(8,128)(2,1)} %bitcast.59, s32[2,256]{1,0:T(2,128)} %wet_any.1), custom_call_target="tpu_custom_call" | custom-call | tf_op jit(solution)/shard_map/pack/pallas_call | solution.py:34
  3.2 0.7 %collective-permute-start.1 = (bf16[272,384]{1,0:T(8,128)(2,1)}, bf16[272,384]{1,0:T(8,128)(2,1)S(1)}, u32[]{:S(2)}, u32[]{:S(2)}) collective-permute-start(bf16[272,384]{1,0:T(8,128)(2,1)} %get-tuple-element.61), channel_id=1, source_target_pairs={{1,2},{2,1},{3,4},{4,3},{5,6},{6,5},{7,8},{8,7},{9,10},{10,9},{11,... | collective-permute-start | bytes 626696 | tf_op jit(solution)/shard_map/ppermute | solution.py:592
  3.9 2.6 %collective-permute-start.3 = (bf16[256,384]{1,0:T(8,128)(2,1)}, bf16[256,384]{1,0:T(8,128)(2,1)S(1)}, u32[]{:S(2)}, u32[]{:S(2)}) collective-permute-start(bf16[256,384]{1,0:T(8,128)(2,1)} %get-tuple-element.71), channel_id=1, source_target_pairs={{0,16},{16,0},{1,17},{17,1},{2,18},{18,2},{3,19},{19,3},{4,20},{20... | collective-permute-start | bytes 589832 | tf_op jit(solution)/shard_map/ppermute | solution.py:587
  6.4 1.5 %copy-done = bf16[2,3,3,192,192]{4,3,2,1,0:T(8,128)(2,1)S(1)} copy-done((bf16[2,3,3,192,192]{4,3,2,1,0:T(8,128)(2,1)S(1)}, bf16[2,3,3,192,192]{4,3,2,1,0:T(8,128)(2,1)}, u32[]{:S(2)}) %copy-start) | copy-done | bytes 1327128
  7.9 1.0 %copy-done.1 = bf16[528,384]{1,0:T(8,128)(2,1)S(1)} copy-done((bf16[528,384]{1,0:T(8,128)(2,1)S(1)}, bf16[528,384]{1,0:T(8,128)(2,1)}, u32[]{:S(2)}) %copy-start.1) | copy-done | bytes 405528
  10.0 2.0 %collective-permute-start.2 = (f32[4,512]{1,0:T(4,128)S(1)}, f32[4,512]{1,0:T(4,128)S(1)}, u32[]{:S(2)}, u32[]{:S(2)}) collective-permute-start(f32[4,512]{1,0:T(4,128)S(1)} %get-tuple-element.64.sent_ref), channel_id=1, source_target_pairs={{0,16},{16,0},{1,17},{17,1},{2,18},{18,2},{3,19},{19,3},{4,20},{20... | collective-permute-start | bytes 24584 | tf_op jit(solution)/shard_map/ppermute | solution.py:587
  12.1 0.9 %back.1.back_ref = f32[256,384]{1,0:T(8,128)S(1)} custom-call(bf16[512,384]{1,0:T(8,128)(2,1)S(1)} %get-tuple-element.65.gpad_ref, bf16[18,384,384]{2,1,0:T(8,128)(2,1)S(1)} %get-tuple-element.66.atmos_ref, bf16[18,256,192]{2,1,0:T(8,128)(2,1)S(1)} %get-tuple-element.67.ocean_ref), custom_call_target="tpu_custom_call" | custom-call | flops 2717908992 | bytes 2654208 | tf_op jit(solution)/shard_map/back/pallas_call | solution.py:34
  13.1 0.7 %collective-permute-done.2.arrived_ref = f32[4,512]{1,0:T(4,128)S(1)} collective-permute-done((f32[4,512]{1,0:T(4,128)S(1)}, f32[4,512]{1,0:T(4,128)S(1)}, u32[]{:S(2)}, u32[]{:S(2)}) %collective-permute-start.2) | collective-permute-done | bytes 8224 | tf_op jit(solution)/shard_map/ppermute | solution.py:587
  13.7 2.1 %first.1 = (bf16[512,384]{1,0:T(8,128)(2,1)S(1)}, bf16[256,384]{1,0:T(8,128)(2,1)S(1)}, bf16[256,384]{1,0:T(8,128)(2,1)S(1)}, bf16[256,384]{1,0:T(8,128)(2,1)S(1)}, bf16[256,384]{1,0:T(8,128)(2,1)S(1)}) custom-call(bf16[512,384]{1,0:T(8,128)(2,1)S(1)} %get-tuple-element.62.xpad_ref, f32[8,512]{1,0:T(8,128)S(1)} %get-tuple-element.63.wet_ref, ...), custom_call_target="tpu_custom_call" | custom-call | flops 2717908992 | bytes 2654208 | tf_op jit(solution)/shard_map/first/pallas_call | solution.py:34
  15.9 0.7 %collective-permute-start.6 = (bf16[256,384]{1,0:T(8,128)(2,1)S(1)}, bf16[256,384]{1,0:T(8,128)(2,1)S(1)}, u32[]{:S(2)}, u32[]{:S(2)}) collective-permute-start(bf16[256,384]{1,0:T(8,128)(2,1)S(1)} %get-tuple-element.79), channel_id=1, source_target_pairs={{1,2},{2,1},{3,4},{4,3},{5,6},{6,5},{7,8},{8,7},{9,10},{10,9},{11,... | collective-permute-start | bytes 589832 | tf_op jit(solution)/shard_map/ppermute | solution.py:592
  16.5 2.2 %collective-permute-start.5 = (bf16[256,384]{1,0:T(8,128)(2,1)S(1)}, bf16[256,384]{1,0:T(8,128)(2,1)S(1)}, u32[]{:S(2)}, u32[]{:S(2)}) collective-permute-start(bf16[256,384]{1,0:T(8,128)(2,1)S(1)} %get-tuple-element.69.give_ref), channel_id=1, source_target_pairs={{0,16},{16,0},{1,17},{17,1},{2,18},{18,2},{3,19},{19,3},{4,20},{20... | collective-permute-start | bytes 589832 | tf_op jit(solution)/shard_map/ppermute | solution.py:587
  18.8 2.3 %own_grads.1 = (f32[3456,384]{1,0:T(8,128)S(1)}, f32[2,1736,128]{2,1,0:T(8,128)S(1)}, bf16[3,384,512]{2,1,0:T(8,128)(2,1)S(1)}) custom-call(bf16[512,384]{1,0:T(8,128)(2,1)S(1)} %get-tuple-element.70.upad_ref, bf16[512,384]{1,0:T(8,128)(2,1)S(1)} %get-tuple-element.65.gpad_ref, bf16[256,384]{1,0:T(8,128)(2,1)S(1)} %get-tuple-element.68.stay_ref, ...), custom_call_target="tpu_custom_call" | custom-call | flops 2717908992 | bytes 2654208 | tf_op jit(solution)/shard_map/own_grads/pallas_call | solution.py:34
  21.1 1.3 %collective-permute-done.5.late_ref = bf16[256,384]{1,0:T(8,128)(2,1)S(1)} collective-permute-done((bf16[256,384]{1,0:T(8,128)(2,1)S(1)}, bf16[256,384]{1,0:T(8,128)(2,1)S(1)}, u32[]{:S(2)}, u32[]{:S(2)}) %collective-permute-start.5) | collective-permute-done | bytes 196640 | tf_op jit(solution)/shard_map/ppermute | solution.py:587
  22.4 1.1 %other_grads.1 = (f32[3456,384]{1,0:T(8,128)S(1)}, f32[2,1736,128]{2,1,0:T(8,128)S(1)}) custom-call(bf16[3,384,512]{2,1,0:T(8,128)(2,1)S(1)} %get-tuple-element.75.left_ref, bf16[256,384]{1,0:T(8,128)(2,1)S(1)} %collective-permute-done.5.late_ref, bf16[256,384]{1,0:T(8,128)(2,1)S(1)} %collective-permute-done.3.early_ref, ...), custom_call_target="tpu_custom_call" | custom-call | flops 2717908992 | bytes 2654208 | tf_op jit(solution)/shard_map/other_grads/pallas_call | solution.py:34
  23.9 5.8 %collective-permute-start.7 = (bf16[8,304,384]{2,1,0:T(8,128)(2,1)S(1)}, bf16[8,304,384]{2,1,0:T(8,128)(2,1)S(1)}, u32[]{:S(2)}, u32[]{:S(2)}) collective-permute-start(bf16[8,304,384]{2,1,0:T(8,128)(2,1)S(1)} %chunk.2), channel_id=1, source_target_pairs={{0,1},{1,0},{2,3},{3,2},{4,5},{5,4},{6,7},{7,6},{8,9},{9,8},{10,11... | collective-permute-start | bytes 5603336 | tf_op jit(solution)/shard_map/ppermute | solution.py:587
  30.1 3.0 %collective-permute-done.7.near_ref = bf16[8,304,384]{2,1,0:T(8,128)(2,1)S(1)} collective-permute-done((bf16[8,304,384]{2,1,0:T(8,128)(2,1)S(1)}, bf16[8,304,384]{2,1,0:T(8,128)(2,1)S(1)}, u32[]{:S(2)}, u32[]{:S(2)}) %collective-permute-start.7) | collective-permute-done | bytes 1867808 | tf_op jit(solution)/shard_map/ppermute | solution.py:587
  33.3 2.3 %collective-permute-start.9 = (bf16[2,2,96,384]{3,2,1,0:T(8,128)(2,1)S(1)}, bf16[2,2,96,384]{3,2,1,0:T(8,128)(2,1)S(1)}, u32[]{:S(2)}, u32[]{:S(2)}) collective-permute-start(bf16[2,2,96,384]{3,2,1,0:T(8,128)(2,1)S(1)} %get-tuple-element.85), channel_id=1, source_target_pairs={{0,4},{1,5},{2,6},{3,7},{4,0},{5,1},{6,2},{7,3},{8,12},{9,13},{10,... | collective-permute-start | bytes 884744 | tf_op jit(solution)/shard_map/ppermute | solution.py:587
  35.6 2.6 %collective-permute-start.10 = (bf16[4,1,96,384]{3,2,1,0:T(8,128)(2,1)S(1)}, bf16[4,1,96,384]{3,2,1,0:T(8,128)(2,1)S(1)}, u32[]{:S(2)}, u32[]{:S(2)}) collective-permute-start(bf16[4,1,96,384]{3,2,1,0:T(8,128)(2,1)S(1)} %get-tuple-element.90), channel_id=1, source_target_pairs={{0,2},{1,3},{2,0},{3,1},{4,6},{5,7},{6,4},{7,5},{8,10},{9,11},{10,... | collective-permute-start | bytes 884744 | tf_op jit(solution)/shard_map/ppermute | solution.py:587
  38.2 1.4 %input_grad.1 = (f32[256,384]{1,0:T(8,128)S(1)}, f32[4,256]{1,0:T(4,128)S(1)}) custom-call(bf16[256,384]{1,0:T(8,128)(2,1)S(1)} %get-tuple-element.68.stay_ref, bf16[256,384]{1,0:T(8,128)(2,1)S(1)} %get-tuple-element.69.give_ref, bf16[8,304,384]{2,1,0:T(8,128)(2,1)S(1)} %collective-permute-done.7.near_ref, ...), custom_call_target="tpu_custom_call" | custom-call | flops 2717908992 | bytes 2654208 | tf_op jit(solution)/shard_map/input_grad/pallas_call | solution.py:34
  39.6 2.0 %collective-permute-start.8 = (f32[4,256]{1,0:T(4,128)S(1)}, f32[4,256]{1,0:T(4,128)S(1)}, u32[]{:S(2)}, u32[]{:S(2)}) collective-permute-start(f32[4,256]{1,0:T(4,128)S(1)} %get-tuple-element.83), channel_id=1, source_target_pairs={{0,16},{16,0},{1,17},{17,1},{2,18},{18,2},{3,19},{19,3},{4,20},{20... | collective-permute-start | bytes 12296 | tf_op jit(solution)/shard_map/ppermute | solution.py:587
  41.6 1.7 %next.1 = (bf16[2,128,384]{2,1,0:T(8,128)(2,1)}, f32[8,128]{1,0:T(8,128)S(1)}) custom-call(bf16[256,384]{1,0:T(8,128)(2,1)S(1)} %get-tuple-element.68.stay_ref, bf16[256,384]{1,0:T(8,128)(2,1)S(1)} %get-tuple-element.69.give_ref, bf16[8,304,384]{2,1,0:T(8,128)(2,1)S(1)} %collective-permute-done.7.near_ref, ...), custom_call_target="tpu_custom_call" | custom-call | flops 2717908992 | bytes 2654208 | tf_op jit(solution)/shard_map/next/pallas_call | solution.py:34
  43.6 2.6 %collective-permute-start.12 = (bf16[1,2,96,384]{3,2,1,0:T(8,128)(2,1)S(1)}, bf16[1,2,96,384]{3,2,1,0:T(8,128)(2,1)S(1)}, u32[]{:S(2)}, u32[]{:S(2)}) collective-permute-start(bf16[1,2,96,384]{3,2,1,0:T(8,128)(2,1)S(1)} %get-tuple-element.95), channel_id=1, source_target_pairs={{0,8},{1,9},{2,10},{3,11},{4,12},{5,13},{6,14},{7,15},{8,0},{9,1},... | collective-permute-start | bytes 442376 | tf_op jit(solution)/shard_map/ppermute | solution.py:587
  46.2 1.2 %last.1 = (bf16[2,128,384]{2,1,0:T(8,128)(2,1)}, f32[8,128]{1,0:T(8,128)S(1)}) custom-call(f32[256,384]{1,0:T(8,128)S(1)} %get-tuple-element.82.grad_ref, f32[4,256]{1,0:T(4,128)S(1)} %collective-permute-done.8.refs_0_.arrived_ref, f32[8,512]{1,0:T(8,128)S(1)} %get-tuple-element.63.wet_ref, f32[16,384]{1,0:T(8,128)S(1)} %fusion.9.terms_ref, ...), custom_call_target="tpu_custom_call" | custom-call | tf_op jit(solution)/shard_map/last/pallas_call | solution.py:34
  47.6 1.6 %collective-permute-start.11 = (bf16[2,1,96,384]{3,2,0,1:T(8,128)(2,1)S(1)}, bf16[2,1,96,384]{3,2,0,1:T(8,128)(2,1)S(1)}, u32[]{:S(2)}, u32[]{:S(2)}) collective-permute-start(bf16[2,1,96,384]{3,2,0,1:T(8,128)(2,1)S(1)} %bitcast.55), channel_id=1, source_target_pairs={{0,4},{1,5},{2,6},{3,7},{4,0},{5,1},{6,2},{7,3},{8,12},{9,13},{10,... | collective-permute-start | bytes 442376 | tf_op jit(solution)/shard_map/ppermute | solution.py:587
  49.1 1.4 %collective-permute-done.13 = bf16[4,1,80,384]{3,2,1,0:T(8,128)(2,1)S(1)} collective-permute-done((bf16[4,1,80,384]{3,2,1,0:T(8,128)(2,1)S(1)}, bf16[4,1,80,384]{3,2,1,0:T(8,128)(2,1)S(1)}, u32[]{:S(2)}, u32[]{:S(2)}) %collective-permute-start.13) | collective-permute-done | bytes 245792 | tf_op jit(solution)/shard_map/ppermute | solution.py:587
  51.1 2.0 %collective-permute-done.12 = bf16[1,2,96,384]{3,2,1,0:T(8,128)(2,1)S(1)} collective-permute-done((bf16[1,2,96,384]{3,2,1,0:T(8,128)(2,1)S(1)}, bf16[1,2,96,384]{3,2,1,0:T(8,128)(2,1)S(1)}, u32[]{:S(2)}, u32[]{:S(2)}) %collective-permute-start.12) | collective-permute-done | bytes 147488 | tf_op jit(solution)/shard_map/ppermute | solution.py:587
  53.1 2.1 %collective-permute-start.15 = (bf16[1,1,96,384]{3,2,1,0:T(8,128)(2,1)S(1)}, bf16[1,1,96,384]{3,2,1,0:T(8,128)(2,1)S(1)}, u32[]{:S(2)}, u32[]{:S(2)}) collective-permute-start(bf16[1,1,96,384]{3,2,1,0:T(8,128)(2,1)S(1)} %get-tuple-element.104), channel_id=1, source_target_pairs={{0,2},{1,3},{2,0},{3,1},{4,6},{5,7},{6,4},{7,5},{8,10},{9,11},{10,... | collective-permute-start | bytes 221192 | tf_op jit(solution)/shard_map/ppermute | solution.py:587
  55.7 0.5 collective-permute-start.14
  56.2 1.0 %collective-permute-done.16 = bf16[2,1,80,384]{3,2,0,1:T(8,128)(2,1)S(1)} collective-permute-done((bf16[2,1,80,384]{3,2,0,1:T(8,128)(2,1)S(1)}, bf16[2,1,80,384]{3,2,0,1:T(8,128)(2,1)S(1)}, u32[]{:S(2)}, u32[]{:S(2)}) %collective-permute-start.16) | collective-permute-done | bytes 122912 | tf_op jit(solution)/shard_map/ppermute | solution.py:587
  57.3 1.5 %collective-permute-start.17 = (bf16[1,1,80,384]{3,2,1,0:T(8,128)(2,1)S(1)}, bf16[1,1,80,384]{3,2,1,0:T(8,128)(2,1)S(1)}, u32[]{:S(2)}, u32[]{:S(2)}) collective-permute-start(bf16[1,1,80,384]{3,2,1,0:T(8,128)(2,1)S(1)} %get-tuple-element.109), channel_id=1, source_target_pairs={{0,8},{1,9},{2,10},{3,11},{4,12},{5,13},{6,14},{7,15},{8,0},{9,1},... | collective-permute-start | bytes 184328 | tf_op jit(solution)/shard_map/ppermute | solution.py:587
  58.8 5.3 %collective-permute-done.17 = bf16[1,1,80,384]{3,2,1,0:T(8,128)(2,1)S(1)} collective-permute-done((bf16[1,1,80,384]{3,2,1,0:T(8,128)(2,1)S(1)}, bf16[1,1,80,384]{3,2,1,0:T(8,128)(2,1)S(1)}, u32[]{:S(2)}, u32[]{:S(2)}) %collective-permute-start.17) | collective-permute-done | bytes 61472 | tf_op jit(solution)/shard_map/ppermute | solution.py:587
  64.1 0.8 %finish.1 = (f32[648,128]{1,0:T(8,128)}, f32[162,128]{1,0:T(8,128)}) custom-call(bf16[96,384]{1,0:T(8,128)(2,1)S(1)} %bitcast.51, bf16[96,384]{1,0:T(8,128)(2,1)S(1)} %bitcast.52, bf16[96,384]{1,0:T(8,128)(2,1)S(1)} %bitcast.49, bf16[96,384]{1,0:T(8,128)(2,1)S(1)} %bitcast.50, bf16[80,384]{1,0:T(8,128)(2,1)S(1)} %bitcast.53, bf16[80,384]{1,0:T(8,128)(2,1)S(1)} %bitcast.54), custom_call_target="tpu_custom_call" | custom-call | tf_op jit(solution)/shard_map/finish/pallas_call | solution.py:34
  (39 shorter events, 4.2 us)
Async XLA Ops:
  2.7 7.1 %collective-permute-start = (bf16[272,384]{1,0:T(8,128)(2,1)}, bf16[272,384]{1,0:T(8,128)(2,1)S(1)}, u32[]{:S(2)}, u32[]{:S(2)}) collective-permute-start(bf16[272,384]{1,0:T(8,128)(2,1)} %get-tuple-element.60), channel_id=1, source_target_pairs={{0,1},{1,0},{2,3},{3,2},{4,5},{5,4},{6,7},{7,6},{8,9},{9,8},{10,11... | collective-permute-start | bytes 626696 | tf_op jit(solution)/shard_map/ppermute | solution.py:587
  3.2 6.5 %collective-permute-start.1 = (bf16[272,384]{1,0:T(8,128)(2,1)}, bf16[272,384]{1,0:T(8,128)(2,1)S(1)}, u32[]{:S(2)}, u32[]{:S(2)}) collective-permute-start(bf16[272,384]{1,0:T(8,128)(2,1)} %get-tuple-element.61), channel_id=1, source_target_pairs={{1,2},{2,1},{3,4},{4,3},{5,6},{6,5},{7,8},{8,7},{9,10},{10,9},{11,... | collective-permute-start | bytes 626696 | tf_op jit(solution)/shard_map/ppermute | solution.py:592
  3.9 14.9 %collective-permute-start.3 = (bf16[256,384]{1,0:T(8,128)(2,1)}, bf16[256,384]{1,0:T(8,128)(2,1)S(1)}, u32[]{:S(2)}, u32[]{:S(2)}) collective-permute-start(bf16[256,384]{1,0:T(8,128)(2,1)} %get-tuple-element.71), channel_id=1, source_target_pairs={{0,16},{16,0},{1,17},{17,1},{2,18},{18,2},{3,19},{19,3},{4,20},{20... | collective-permute-start | bytes 589832 | tf_op jit(solution)/shard_map/ppermute | solution.py:587
  6.4 1.5 %copy-start = (bf16[2,3,3,192,192]{4,3,2,1,0:T(8,128)(2,1)S(1)}, bf16[2,3,3,192,192]{4,3,2,1,0:T(8,128)(2,1)}, u32[]{:S(2)}) copy-start(bf16[2,3,3,192,192]{4,3,2,1,0:T(8,128)(2,1)} %param.12) | copy-start | bytes 3981316
  7.9 1.0 %copy-start.1 = (bf16[528,384]{1,0:T(8,128)(2,1)S(1)}, bf16[528,384]{1,0:T(8,128)(2,1)}, u32[]{:S(2)}) copy-start(bf16[528,384]{1,0:T(8,128)(2,1)} %get-tuple-element.58.own_in) | copy-start | bytes 1216516
  8.9 0.7 %copy-start.2 = (bf16[4,384]{1,0:T(4,128)(2,1)S(1)}, bf16[4,384]{1,0:T(4,128)(2,1)}, u32[]{:S(2)}) copy-start(bf16[4,384]{1,0:T(4,128)(2,1)} %coupling_ref.1) | copy-start | bytes 9220
  8.9 0.7 %copy-start.3 = (bf16[384,4]{0,1:T(4,128)(2,1)S(1)}, bf16[384,4]{0,1:T(4,128)(2,1)}, u32[]{:S(2)}) copy-start(bf16[384,4]{0,1:T(4,128)(2,1)} %param.16) | copy-start | bytes 9220
  8.9 0.7 %copy-start.4 = (bf16[4,192]{1,0:T(4,128)(2,1)S(1)}, bf16[4,192]{1,0:T(4,128)(2,1)}, u32[]{:S(2)}) copy-start(bf16[4,192]{1,0:T(4,128)(2,1)} %param.15) | copy-start | bytes 4612
  8.9 0.7 %copy-start.5 = (bf16[192,4]{0,1:T(4,128)(2,1)S(1)}, bf16[192,4]{0,1:T(4,128)(2,1)}, u32[]{:S(2)}) copy-start(bf16[192,4]{0,1:T(4,128)(2,1)} %param.14) | copy-start | bytes 4612
  10.0 3.7 %collective-permute-start.2 = (f32[4,512]{1,0:T(4,128)S(1)}, f32[4,512]{1,0:T(4,128)S(1)}, u32[]{:S(2)}, u32[]{:S(2)}) collective-permute-start(f32[4,512]{1,0:T(4,128)S(1)} %get-tuple-element.64.sent_ref), channel_id=1, source_target_pairs={{0,16},{16,0},{1,17},{17,1},{2,18},{18,2},{3,19},{19,3},{4,20},{20... | collective-permute-start | bytes 24584 | tf_op jit(solution)/shard_map/ppermute | solution.py:587
  12.0 6.8 %collective-permute-start.4 = (bf16[256,384]{1,0:T(8,128)(2,1)S(1)}, bf16[256,384]{1,0:T(8,128)(2,1)S(1)}, u32[]{:S(2)}, u32[]{:S(2)}) collective-permute-start(bf16[256,384]{1,0:T(8,128)(2,1)S(1)} %get-tuple-element.72), channel_id=1, source_target_pairs={{0,16},{16,0},{1,17},{17,1},{2,18},{18,2},{3,19},{19,3},{4,20},{20... | collective-permute-start | bytes 589832 | tf_op jit(solution)/shard_map/ppermute | solution.py:587
  15.9 7.7 %collective-permute-start.6 = (bf16[256,384]{1,0:T(8,128)(2,1)S(1)}, bf16[256,384]{1,0:T(8,128)(2,1)S(1)}, u32[]{:S(2)}, u32[]{:S(2)}) collective-permute-start(bf16[256,384]{1,0:T(8,128)(2,1)S(1)} %get-tuple-element.79), channel_id=1, source_target_pairs={{1,2},{2,1},{3,4},{4,3},{5,6},{6,5},{7,8},{8,7},{9,10},{10,9},{11,... | collective-permute-start | bytes 589832 | tf_op jit(solution)/shard_map/ppermute | solution.py:592
  16.5 5.9 %collective-permute-start.5 = (bf16[256,384]{1,0:T(8,128)(2,1)S(1)}, bf16[256,384]{1,0:T(8,128)(2,1)S(1)}, u32[]{:S(2)}, u32[]{:S(2)}) collective-permute-start(bf16[256,384]{1,0:T(8,128)(2,1)S(1)} %get-tuple-element.69.give_ref), channel_id=1, source_target_pairs={{0,16},{16,0},{1,17},{17,1},{2,18},{18,2},{3,19},{19,3},{4,20},{20... | collective-permute-start | bytes 589832 | tf_op jit(solution)/shard_map/ppermute | solution.py:587
  23.9 9.2 %collective-permute-start.7 = (bf16[8,304,384]{2,1,0:T(8,128)(2,1)S(1)}, bf16[8,304,384]{2,1,0:T(8,128)(2,1)S(1)}, u32[]{:S(2)}, u32[]{:S(2)}) collective-permute-start(bf16[8,304,384]{2,1,0:T(8,128)(2,1)S(1)} %chunk.2), channel_id=1, source_target_pairs={{0,1},{1,0},{2,3},{3,2},{4,5},{5,4},{6,7},{7,6},{8,9},{9,8},{10,11... | collective-permute-start | bytes 5603336 | tf_op jit(solution)/shard_map/ppermute | solution.py:587
  33.3 10.2 %collective-permute-start.9 = (bf16[2,2,96,384]{3,2,1,0:T(8,128)(2,1)S(1)}, bf16[2,2,96,384]{3,2,1,0:T(8,128)(2,1)S(1)}, u32[]{:S(2)}, u32[]{:S(2)}) collective-permute-start(bf16[2,2,96,384]{3,2,1,0:T(8,128)(2,1)S(1)} %get-tuple-element.85), channel_id=1, source_target_pairs={{0,4},{1,5},{2,6},{3,7},{4,0},{5,1},{6,2},{7,3},{8,12},{9,13},{10,... | collective-permute-start | bytes 884744 | tf_op jit(solution)/shard_map/ppermute | solution.py:587
  35.6 11.8 %collective-permute-start.10 = (bf16[4,1,96,384]{3,2,1,0:T(8,128)(2,1)S(1)}, bf16[4,1,96,384]{3,2,1,0:T(8,128)(2,1)S(1)}, u32[]{:S(2)}, u32[]{:S(2)}) collective-permute-start(bf16[4,1,96,384]{3,2,1,0:T(8,128)(2,1)S(1)} %get-tuple-element.90), channel_id=1, source_target_pairs={{0,2},{1,3},{2,0},{3,1},{4,6},{5,7},{6,4},{7,5},{8,10},{9,11},{10,... | collective-permute-start | bytes 884744 | tf_op jit(solution)/shard_map/ppermute | solution.py:587
  39.6 3.9 %collective-permute-start.8 = (f32[4,256]{1,0:T(4,128)S(1)}, f32[4,256]{1,0:T(4,128)S(1)}, u32[]{:S(2)}, u32[]{:S(2)}) collective-permute-start(f32[4,256]{1,0:T(4,128)S(1)} %get-tuple-element.83), channel_id=1, source_target_pairs={{0,16},{16,0},{1,17},{17,1},{2,18},{18,2},{3,19},{19,3},{4,20},{20... | collective-permute-start | bytes 12296 | tf_op jit(solution)/shard_map/ppermute | solution.py:587
  41.6 8.9 %collective-permute-start.13 = (bf16[4,1,80,384]{3,2,1,0:T(8,128)(2,1)S(1)}, bf16[4,1,80,384]{3,2,1,0:T(8,128)(2,1)S(1)}, u32[]{:S(2)}, u32[]{:S(2)}) collective-permute-start(bf16[4,1,80,384]{3,2,1,0:T(8,128)(2,1)S(1)} %get-tuple-element.97), channel_id=1, source_target_pairs={{0,2},{1,3},{2,0},{3,1},{4,6},{5,7},{6,4},{7,5},{8,10},{9,11},{10,... | collective-permute-start | bytes 737288 | tf_op jit(solution)/shard_map/ppermute | solution.py:587
  43.6 9.4 %collective-permute-start.12 = (bf16[1,2,96,384]{3,2,1,0:T(8,128)(2,1)S(1)}, bf16[1,2,96,384]{3,2,1,0:T(8,128)(2,1)S(1)}, u32[]{:S(2)}, u32[]{:S(2)}) collective-permute-start(bf16[1,2,96,384]{3,2,1,0:T(8,128)(2,1)S(1)} %get-tuple-element.95), channel_id=1, source_target_pairs={{0,8},{1,9},{2,10},{3,11},{4,12},{5,13},{6,14},{7,15},{8,0},{9,1},... | collective-permute-start | bytes 442376 | tf_op jit(solution)/shard_map/ppermute | solution.py:587
  47.6 8.1 %collective-permute-start.11 = (bf16[2,1,96,384]{3,2,0,1:T(8,128)(2,1)S(1)}, bf16[2,1,96,384]{3,2,0,1:T(8,128)(2,1)S(1)}, u32[]{:S(2)}, u32[]{:S(2)}) collective-permute-start(bf16[2,1,96,384]{3,2,0,1:T(8,128)(2,1)S(1)} %bitcast.55), channel_id=1, source_target_pairs={{0,4},{1,5},{2,6},{3,7},{4,0},{5,1},{6,2},{7,3},{8,12},{9,13},{10,... | collective-permute-start | bytes 442376 | tf_op jit(solution)/shard_map/ppermute | solution.py:587
  50.6 6.7 %collective-permute-start.16 = (bf16[2,1,80,384]{3,2,0,1:T(8,128)(2,1)S(1)}, bf16[2,1,80,384]{3,2,0,1:T(8,128)(2,1)S(1)}, u32[]{:S(2)}, u32[]{:S(2)}) collective-permute-start(bf16[2,1,80,384]{3,2,0,1:T(8,128)(2,1)S(1)} %bitcast.56), channel_id=1, source_target_pairs={{0,4},{1,5},{2,6},{3,7},{4,0},{5,1},{6,2},{7,3},{8,12},{9,13},{10,... | collective-permute-start | bytes 368648 | tf_op jit(solution)/shard_map/ppermute | solution.py:587
  53.1 11.0 %collective-permute-start.15 = (bf16[1,1,96,384]{3,2,1,0:T(8,128)(2,1)S(1)}, bf16[1,1,96,384]{3,2,1,0:T(8,128)(2,1)S(1)}, u32[]{:S(2)}, u32[]{:S(2)}) collective-permute-start(bf16[1,1,96,384]{3,2,1,0:T(8,128)(2,1)S(1)} %get-tuple-element.104), channel_id=1, source_target_pairs={{0,2},{1,3},{2,0},{3,1},{4,6},{5,7},{6,4},{7,5},{8,10},{9,11},{10,... | collective-permute-start | bytes 221192 | tf_op jit(solution)/shard_map/ppermute | solution.py:587
  55.7 8.4 %collective-permute-start.14 = (bf16[1,1,96,384]{3,2,1,0:T(8,128)(2,1)S(1)}, bf16[1,1,96,384]{3,2,1,0:T(8,128)(2,1)S(1)}, u32[]{:S(2)}, u32[]{:S(2)}) collective-permute-start(bf16[1,1,96,384]{3,2,1,0:T(8,128)(2,1)S(1)} %get-tuple-element.102), channel_id=1, source_target_pairs={{0,8},{1,9},{2,10},{3,11},{4,12},{5,13},{6,14},{7,15},{8,0},{9,1},... | collective-permute-start | bytes 221192 | tf_op jit(solution)/shard_map/ppermute | solution.py:587
  57.3 6.8 %collective-permute-start.17 = (bf16[1,1,80,384]{3,2,1,0:T(8,128)(2,1)S(1)}, bf16[1,1,80,384]{3,2,1,0:T(8,128)(2,1)S(1)}, u32[]{:S(2)}, u32[]{:S(2)}) collective-permute-start(bf16[1,1,80,384]{3,2,1,0:T(8,128)(2,1)S(1)} %get-tuple-element.109), channel_id=1, source_target_pairs={{0,8},{1,9},{2,10},{3,11},{4,12},{5,13},{6,14},{7,15},{8,0},{9,1},... | collective-permute-start | bytes 184328 | tf_op jit(solution)/shard_map/ppermute | solution.py:587

commit v2 on v1

--- a/solution.py
+++ b/solution.py
@@ -348,7 +348,8 @@
 
 
 def hidden_and_grad(stay_ref, give_ref):
-    stay, give = stay_ref[...], give_ref[...]
+    stay = stay_ref[...]
+    give = give_ref[0 : stay.shape[0], :]
     return jnp.where(on_ocean(), give, stay), jnp.where(on_ocean(), stay, give)
 
 
@@ -378,18 +379,18 @@
 
 
 def other_grads_kernel(left_ref, late_ref, early_ref, edge_ref, atmos_out, ocean_out, *, cols):
-    rows = late_ref.shape[0]
+    rows = early_ref.shape[0]
 
     @pl.when(on_ocean())
     def _():
         store = store_into(atmos_out)
         for tap in range(9):
             start = cols * (tap // 3)
-            store(tap, dot(left_ref[tap % 3, :, start : start + rows], late_ref[...]))
+            store(tap, dot(left_ref[tap % 3, :, start : start + rows], late_ref[0:rows, :]))
 
     @pl.when(jnp.logical_not(on_ocean()))
     def _():
-        late = late_ref[...].astype(F32)
+        late = late_ref[0:rows, :].astype(F32)
         grad_ocean(whole_pad(early_ref, edge_ref, cols), late, False, cols, store_into(ocean_out))
 
 
@@ -477,9 +478,33 @@
     )
 
 
+def halve_both_kernel(a_keep, a_came, b_keep, b_came, *refs, bits):
+    for index, (pair, bit) in enumerate((((a_keep, a_came), bits[0]), ((b_keep, b_came), bits[1]))):
+        own = own_bit(bit)
+        keep_out, send_out = refs[2 * index - 5 : 2 * index - 3]
+        halve(*pair, send_out, 1 - own, slice(None))
+        halve(*pair, keep_out, own, slice(None))
+    refs[-1][...] = jnp.zeros_like(refs[-1])
+
+
+def halved_both(a_keep, a_came, a_bit, b_keep, b_came, b_bit, after):
+    inputs, outs = [], []
+    for keep, came in ((a_keep, a_came), (b_keep, b_came)):
+        rows, channels = keep.shape[-2:]
+        inputs += [part.reshape(1, 2, 1, rows, channels) for part in (keep, came)]
+        outs += [shape((1, 1, rows, channels), BF16)] * 2
+    return call(
+        functools.partial(halve_both_kernel, bits=(a_bit, b_bit)),
+        [*outs, MARK],
+        [*inputs, after],
+        [WHOLE] * 4 + [ANYWHERE],
+        name="halve_both",
+    )
+
+
 def split(keep, came):
     pairs, tall, channels = keep.shape
-    cuts = [16 * (tall // 16 * part // 17) for part in (6, 6)]
+    cuts = [16 * (tall // 16 * part // 17) for part in (6, 7)]
     cuts.append(tall - sum(cuts))
     outs = [
         shape(((2, 2) if index == 1 else (4, 1)) + (rows, channels), BF16) for index, rows in enumerate(cuts)
@@ -511,10 +536,9 @@
     a_came = swapped(a_send, "lat", 4)
     c_keep, c_send, mark = halved(c_keep, c_came, 2, (2, 1), [mark])
     c_came = swapped(c_send, "lat", 4)
-    b_keep, b_send, mark = halved(b_keep, b_came, 1, (1, 1), [mark])
+    a_keep, a_send, b_keep, b_send, mark = halved_both(a_keep, a_came, 3, b_keep, b_came, 1, mark)
+    a_came = swapped(a_send, "lat", 8)
     b_came = swapped(b_send, "lat", 2)
-    a_keep, a_send, mark = halved(a_keep, a_came, 3, (1, 1), [mark])
-    a_came = swapped(a_send, "lat", 8)
     c_keep, c_send = halved(c_keep, c_came, 3, (1, 1), [mark], False)
     c_came = swapped(c_send, "lat", 8)
     return [part.reshape(-1, channels) for part in (a_keep, a_came, b_keep, b_came, c_keep, c_came)]

time: 65.2 us -> 66.7 us (1.023)
  waiting for transfers between devices: 15.1 us -> 17.5 us
  starting transfers between devices: 30.3 us -> 29.5 us
    ppermute x16, waiting for transfers between devices: 15.1 us -> 17.4 us  [swapped(): return lax.ppermute(value, axis, pairs)]
    ppermute x16, starting transfers between devices: 29 us -> 28.2 us  [swapped(): return lax.ppermute(value, axis, pairs)]
    pallas_call x21 -> x20, Pallas kernels: 15.7 us -> 15.6 us  [call(): pl.pallas_call(kernel, out_shape=outs, in_specs=in_specs or [WHOLE] * len...]
  transfers between devices with their start and end apart: 18 -> 18, of which waited for: 8 -> 7; matrix products, arithmetic and copies ran while one was open for 0% -> 0% of each run, Pallas kernels for 19% -> 18%
where the time goes in v2:
time: 66.7 us; the launch traced here: 66.4 us
  starting transfers between devices  29.5 us (44%)
  waiting for transfers between devices  17.5 us (26%)
  Pallas kernels  15.6 us (23%)
  local copies, waits for them, and re-layouts  2.97 us (4%)
  between operations  0.79 us (1%)
    ppermute x16, starting transfers between devices, swapped(): return lax.ppermute(value, axis, pairs)  28.2 us
    ppermute x16, waiting for transfers between devices, swapped(): return lax.ppermute(value, axis, pairs)  17.4 us
    pallas_call x20, Pallas kernels, call(): pl.pallas_call(kernel, out_shape=outs, in_specs=in_specs or [WHOLE] * len...  15.6 us
    unnamed x12, local copies, waits for them, and re-layouts  2.96 us
    ppermute x2, starting transfers between devices, far_halo(): return lax.ppermute(far, 'lat', pairs)  1.34 us
  transfers between devices with their start and end apart: 18, of which 7 were waited for; matrix products, arithmetic and copies ran while one was open for 0% of the time, Pallas kernels for 18%

profile of v2, /device:TPU:0, one launch (start us, length us, event | category | flops | bytes accessed | tf_op | source)
XLA Modules:
  0.0 66.4 jit_solution(13914029764156560143)
XLA Ops:
  0.6 2.0 %pack.1 = (bf16[272,384]{1,0:T(8,128)(2,1)}, bf16[272,384]{1,0:T(8,128)(2,1)}, bf16[256,384]{1,0:T(8,128)(2,1)}, bf16[528,384]{1,0:T(8,128)(2,1)}) custom-call(bf16[2,128,384]{2,1,0:T(8,128)(2,1)} %bitcast.58, bf16[2,128,384]{2,1,0:T(8,128)(2,1)} %bitcast.59, s32[2,256]{1,0:T(2,128)} %wet_any.1), custom_call_target="tpu_custom_call" | custom-call | tf_op jit(solution)/shard_map/pack/pallas_call | solution.py:34
  2.7 0.5 collective-permute-start
  3.2 0.7 collective-permute-start.1
  3.9 2.6 %collective-permute-start.3 = (bf16[256,384]{1,0:T(8,128)(2,1)}, bf16[256,384]{1,0:T(8,128)(2,1)S(1)}, u32[]{:S(2)}, u32[]{:S(2)}) collective-permute-start(bf16[256,384]{1,0:T(8,128)(2,1)} %get-tuple-element.70), channel_id=1, source_target_pairs={{0,16},{16,0},{1,17},{17,1},{2,18},{18,2},{3,19},{19,3},{4,20},{20... | collective-permute-start | bytes 589832 | tf_op jit(solution)/shard_map/ppermute | solution.py:611
  6.4 1.5 %copy-done = bf16[2,3,3,192,192]{4,3,2,1,0:T(8,128)(2,1)S(1)} copy-done((bf16[2,3,3,192,192]{4,3,2,1,0:T(8,128)(2,1)S(1)}, bf16[2,3,3,192,192]{4,3,2,1,0:T(8,128)(2,1)}, u32[]{:S(2)}) %copy-start) | copy-done | bytes 1327128
  7.9 1.0 %copy-done.1 = bf16[528,384]{1,0:T(8,128)(2,1)S(1)} copy-done((bf16[528,384]{1,0:T(8,128)(2,1)S(1)}, bf16[528,384]{1,0:T(8,128)(2,1)}, u32[]{:S(2)}) %copy-start.1) | copy-done | bytes 405528
  10.0 2.0 %collective-permute-start.2 = (f32[4,512]{1,0:T(4,128)S(1)}, f32[4,512]{1,0:T(4,128)S(1)}, u32[]{:S(2)}, u32[]{:S(2)}) collective-permute-start(f32[4,512]{1,0:T(4,128)S(1)} %get-tuple-element.63.sent_ref), channel_id=1, source_target_pairs={{0,16},{16,0},{1,17},{17,1},{2,18},{18,2},{3,19},{19,3},{4,20},{20... | collective-permute-start | bytes 24584 | tf_op jit(solution)/shard_map/ppermute | solution.py:611
  12.1 0.9 %back.1.back_ref = f32[256,384]{1,0:T(8,128)S(1)} custom-call(bf16[512,384]{1,0:T(8,128)(2,1)S(1)} %get-tuple-element.64.gpad_ref, bf16[18,384,384]{2,1,0:T(8,128)(2,1)S(1)} %get-tuple-element.65.atmos_ref, bf16[18,256,192]{2,1,0:T(8,128)(2,1)S(1)} %get-tuple-element.66.ocean_ref), custom_call_target="tpu_custom_call" | custom-call | flops 2717908992 | bytes 2654208 | tf_op jit(solution)/shard_map/back/pallas_call | solution.py:34
  13.1 0.7 %collective-permute-done.2.arrived_ref = f32[4,512]{1,0:T(4,128)S(1)} collective-permute-done((f32[4,512]{1,0:T(4,128)S(1)}, f32[4,512]{1,0:T(4,128)S(1)}, u32[]{:S(2)}, u32[]{:S(2)}) %collective-permute-start.2) | collective-permute-done | bytes 8224 | tf_op jit(solution)/shard_map/ppermute | solution.py:611
  13.7 2.1 %first.1 = (bf16[512,384]{1,0:T(8,128)(2,1)S(1)}, bf16[256,384]{1,0:T(8,128)(2,1)S(1)}, bf16[256,384]{1,0:T(8,128)(2,1)S(1)}, bf16[256,384]{1,0:T(8,128)(2,1)S(1)}, bf16[256,384]{1,0:T(8,128)(2,1)S(1)}) custom-call(bf16[512,384]{1,0:T(8,128)(2,1)S(1)} %get-tuple-element.61.xpad_ref, f32[8,512]{1,0:T(8,128)S(1)} %get-tuple-element.62.wet_ref, ...), custom_call_target="tpu_custom_call" | custom-call | flops 2717908992 | bytes 2654208 | tf_op jit(solution)/shard_map/first/pallas_call | solution.py:34
  15.9 0.7 %collective-permute-start.6 = (bf16[256,384]{1,0:T(8,128)(2,1)S(1)}, bf16[256,384]{1,0:T(8,128)(2,1)S(1)}, u32[]{:S(2)}, u32[]{:S(2)}) collective-permute-start(bf16[256,384]{1,0:T(8,128)(2,1)S(1)} %get-tuple-element.78), channel_id=1, source_target_pairs={{1,2},{2,1},{3,4},{4,3},{5,6},{6,5},{7,8},{8,7},{9,10},{10,9},{11,... | collective-permute-start | bytes 589832 | tf_op jit(solution)/shard_map/ppermute | solution.py:616
  16.5 2.2 %collective-permute-start.5 = (bf16[256,384]{1,0:T(8,128)(2,1)S(1)}, bf16[256,384]{1,0:T(8,128)(2,1)S(1)}, u32[]{:S(2)}, u32[]{:S(2)}) collective-permute-start(bf16[256,384]{1,0:T(8,128)(2,1)S(1)} %get-tuple-element.68.give_ref), channel_id=1, source_target_pairs={{0,16},{16,0},{1,17},{17,1},{2,18},{18,2},{3,19},{19,3},{4,20},{20... | collective-permute-start | bytes 589832 | tf_op jit(solution)/shard_map/ppermute | solution.py:611
  18.8 2.3 %own_grads.1 = (f32[3456,384]{1,0:T(8,128)S(1)}, f32[2,1736,128]{2,1,0:T(8,128)S(1)}, bf16[3,384,512]{2,1,0:T(8,128)(2,1)S(1)}) custom-call(bf16[512,384]{1,0:T(8,128)(2,1)S(1)} %get-tuple-element.69.upad_ref, bf16[512,384]{1,0:T(8,128)(2,1)S(1)} %get-tuple-element.64.gpad_ref, bf16[256,384]{1,0:T(8,128)(2,1)S(1)} %get-tuple-element.67.stay_ref, ...), custom_call_target="tpu_custom_call" | custom-call | flops 2717908992 | bytes 2654208 | tf_op jit(solution)/shard_map/own_grads/pallas_call | solution.py:34
  21.1 1.3 %collective-permute-done.5.late_ref = bf16[256,384]{1,0:T(8,128)(2,1)S(1)} collective-permute-done((bf16[256,384]{1,0:T(8,128)(2,1)S(1)}, bf16[256,384]{1,0:T(8,128)(2,1)S(1)}, u32[]{:S(2)}, u32[]{:S(2)}) %collective-permute-start.5) | collective-permute-done | bytes 196640 | tf_op jit(solution)/shard_map/ppermute | solution.py:611
  22.4 1.1 %other_grads.1 = (f32[3456,384]{1,0:T(8,128)S(1)}, f32[2,1736,128]{2,1,0:T(8,128)S(1)}) custom-call(bf16[3,384,512]{2,1,0:T(8,128)(2,1)S(1)} %get-tuple-element.74.left_ref, bf16[256,384]{1,0:T(8,128)(2,1)S(1)} %collective-permute-done.5.late_ref, bf16[256,384]{1,0:T(8,128)(2,1)S(1)} %collective-permute-done.3.early_ref, ...), custom_call_target="tpu_custom_call" | custom-call | flops 2717908992 | bytes 2654208 | tf_op jit(solution)/shard_map/other_grads/pallas_call | solution.py:34
  23.9 5.8 %collective-permute-start.7 = (bf16[8,304,384]{2,1,0:T(8,128)(2,1)S(1)}, bf16[8,304,384]{2,1,0:T(8,128)(2,1)S(1)}, u32[]{:S(2)}, u32[]{:S(2)}) collective-permute-start(bf16[8,304,384]{2,1,0:T(8,128)(2,1)S(1)} %chunk.2), channel_id=1, source_target_pairs={{0,1},{1,0},{2,3},{3,2},{4,5},{5,4},{6,7},{7,6},{8,9},{9,8},{10,11... | collective-permute-start | bytes 5603336 | tf_op jit(solution)/shard_map/ppermute | solution.py:611
  30.1 3.0 %collective-permute-done.7.near_ref = bf16[8,304,384]{2,1,0:T(8,128)(2,1)S(1)} collective-permute-done((bf16[8,304,384]{2,1,0:T(8,128)(2,1)S(1)}, bf16[8,304,384]{2,1,0:T(8,128)(2,1)S(1)}, u32[]{:S(2)}, u32[]{:S(2)}) %collective-permute-start.7) | collective-permute-done | bytes 1867808 | tf_op jit(solution)/shard_map/ppermute | solution.py:611
  33.3 3.3 %collective-permute-start.10 = (bf16[4,1,96,384]{3,2,1,0:T(8,128)(2,1)S(1)}, bf16[4,1,96,384]{3,2,1,0:T(8,128)(2,1)S(1)}, u32[]{:S(2)}, u32[]{:S(2)}) collective-permute-start(bf16[4,1,96,384]{3,2,1,0:T(8,128)(2,1)S(1)} %get-tuple-element.89), channel_id=1, source_target_pairs={{0,2},{1,3},{2,0},{3,1},{4,6},{5,7},{6,4},{7,5},{8,10},{9,11},{10,... | collective-permute-start | bytes 884744 | tf_op jit(solution)/shard_map/ppermute | solution.py:611
  36.6 1.6 %collective-permute-start.9 = (bf16[2,2,112,384]{3,2,1,0:T(8,128)(2,1)S(1)}, bf16[2,2,112,384]{3,2,1,0:T(8,128)(2,1)S(1)}, u32[]{:S(2)}, u32[]{:S(2)}) collective-permute-start(bf16[2,2,112,384]{3,2,1,0:T(8,128)(2,1)S(1)} %get-tuple-element.84), channel_id=1, source_target_pairs={{0,4},{1,5},{2,6},{3,7},{4,0},{5,1},{6,2},{7,3},{8,12},{9,13},{10,... | collective-permute-start | bytes 1032200 | tf_op jit(solution)/shard_map/ppermute | solution.py:611
  38.2 1.4 %input_grad.1 = (f32[256,384]{1,0:T(8,128)S(1)}, f32[4,256]{1,0:T(4,128)S(1)}) custom-call(bf16[256,384]{1,0:T(8,128)(2,1)S(1)} %get-tuple-element.67.stay_ref, bf16[256,384]{1,0:T(8,128)(2,1)S(1)} %get-tuple-element.68.give_ref, bf16[8,304,384]{2,1,0:T(8,128)(2,1)S(1)} %collective-permute-done.7.near_ref, ...), custom_call_target="tpu_custom_call" | custom-call | flops 2717908992 | bytes 2654208 | tf_op jit(solution)/shard_map/input_grad/pallas_call | solution.py:34
  39.6 2.0 %collective-permute-start.8 = (f32[4,256]{1,0:T(4,128)S(1)}, f32[4,256]{1,0:T(4,128)S(1)}, u32[]{:S(2)}, u32[]{:S(2)}) collective-permute-start(f32[4,256]{1,0:T(4,128)S(1)} %get-tuple-element.82), channel_id=1, source_target_pairs={{0,16},{16,0},{1,17},{17,1},{2,18},{18,2},{3,19},{19,3},{4,20},{20... | collective-permute-start | bytes 12296 | tf_op jit(solution)/shard_map/ppermute | solution.py:611
  41.7 1.7 %next.1 = (bf16[2,128,384]{2,1,0:T(8,128)(2,1)}, f32[8,128]{1,0:T(8,128)S(1)}) custom-call(bf16[256,384]{1,0:T(8,128)(2,1)S(1)} %get-tuple-element.67.stay_ref, bf16[256,384]{1,0:T(8,128)(2,1)S(1)} %get-tuple-element.68.give_ref, bf16[8,304,384]{2,1,0:T(8,128)(2,1)S(1)} %collective-permute-done.7.near_ref, ...), custom_call_target="tpu_custom_call" | custom-call | flops 2717908992 | bytes 2654208 | tf_op jit(solution)/shard_map/next/pallas_call | solution.py:34
  43.6 2.9 %collective-permute-done.9 = bf16[2,2,112,384]{3,2,1,0:T(8,128)(2,1)S(1)} collective-permute-done((bf16[2,2,112,384]{3,2,1,0:T(8,128)(2,1)S(1)}, bf16[2,2,112,384]{3,2,1,0:T(8,128)(2,1)S(1)}, u32[]{:S(2)}, u32[]{:S(2)}) %collective-permute-start.9) | collective-permute-done | bytes 344096 | tf_op jit(solution)/shard_map/ppermute | solution.py:611
  46.6 2.7 %collective-permute-start.12 = (bf16[1,2,112,384]{3,2,1,0:T(8,128)(2,1)S(1)}, bf16[1,2,112,384]{3,2,1,0:T(8,128)(2,1)S(1)}, u32[]{:S(2)}, u32[]{:S(2)}) collective-permute-start(bf16[1,2,112,384]{3,2,1,0:T(8,128)(2,1)S(1)} %get-tuple-element.94), channel_id=1, source_target_pairs={{0,8},{1,9},{2,10},{3,11},{4,12},{5,13},{6,14},{7,15},{8,0},{9,1},... | collective-permute-start | bytes 516104 | tf_op jit(solution)/shard_map/ppermute | solution.py:611
  49.2 1.2 %last.1 = (bf16[2,128,384]{2,1,0:T(8,128)(2,1)}, f32[8,128]{1,0:T(8,128)S(1)}) custom-call(f32[256,384]{1,0:T(8,128)S(1)} %get-tuple-element.81.grad_ref, f32[4,256]{1,0:T(4,128)S(1)} %collective-permute-done.8.refs_0_.arrived_ref, f32[8,512]{1,0:T(8,128)S(1)} %get-tuple-element.62.wet_ref, f32[16,384]{1,0:T(8,128)S(1)} %fusion.9.terms_ref, ...), custom_call_target="tpu_custom_call" | custom-call | tf_op jit(solution)/shard_map/last/pallas_call | solution.py:34
  50.9 1.8 %collective-permute-start.16 = (bf16[2,1,64,384]{3,2,0,1:T(8,128)(2,1)S(1)}, bf16[2,1,64,384]{3,2,0,1:T(8,128)(2,1)S(1)}, u32[]{:S(2)}, u32[]{:S(2)}) collective-permute-start(bf16[2,1,64,384]{3,2,0,1:T(8,128)(2,1)S(1)} %bitcast.56), channel_id=1, source_target_pairs={{0,4},{1,5},{2,6},{3,7},{4,0},{5,1},{6,2},{7,3},{8,12},{9,13},{10,... | collective-permute-start | bytes 294920 | tf_op jit(solution)/shard_map/ppermute | solution.py:611
  52.7 5.9 %collective-permute-done.11 = bf16[2,1,96,384]{3,2,0,1:T(8,128)(2,1)S(1)} collective-permute-done((bf16[2,1,96,384]{3,2,0,1:T(8,128)(2,1)S(1)}, bf16[2,1,96,384]{3,2,0,1:T(8,128)(2,1)S(1)}, u32[]{:S(2)}, u32[]{:S(2)}) %collective-permute-start.11) | collective-permute-done | bytes 147488 | tf_op jit(solution)/shard_map/ppermute | solution.py:611
  58.8 0.7 %collective-permute-start.15 = (bf16[1,1,112,384]{3,2,1,0:T(8,128)(2,1)S(1)}, bf16[1,1,112,384]{3,2,1,0:T(8,128)(2,1)S(1)}, u32[]{:S(2)}, u32[]{:S(2)}) collective-permute-start(bf16[1,1,112,384]{3,2,1,0:T(8,128)(2,1)S(1)} %get-tuple-element.102), channel_id=1, source_target_pairs={{0,2},{1,3},{2,0},{3,1},{4,6},{5,7},{6,4},{7,5},{8,10},{9,11},{10,... | collective-permute-start | bytes 258056 | tf_op jit(solution)/shard_map/ppermute | solution.py:611
  59.5 0.6 collective-permute-done.16
  60.1 2.4 %collective-permute-start.17 = (bf16[1,1,64,384]{3,2,1,0:T(8,128)(2,1)S(1)}, bf16[1,1,64,384]{3,2,1,0:T(8,128)(2,1)S(1)}, u32[]{:S(2)}, u32[]{:S(2)}) collective-permute-start(bf16[1,1,64,384]{3,2,1,0:T(8,128)(2,1)S(1)} %get-tuple-element.107), channel_id=1, source_target_pairs={{0,8},{1,9},{2,10},{3,11},{4,12},{5,13},{6,14},{7,15},{8,0},{9,1},... | collective-permute-start | bytes 147464 | tf_op jit(solution)/shard_map/ppermute | solution.py:611
  62.5 3.1 %collective-permute-done.17 = bf16[1,1,64,384]{3,2,1,0:T(8,128)(2,1)S(1)} collective-permute-done((bf16[1,1,64,384]{3,2,1,0:T(8,128)(2,1)S(1)}, bf16[1,1,64,384]{3,2,1,0:T(8,128)(2,1)S(1)}, u32[]{:S(2)}, u32[]{:S(2)}) %collective-permute-start.17) | collective-permute-done | bytes 49184 | tf_op jit(solution)/shard_map/ppermute | solution.py:611
  65.6 0.8 %finish.1 = (f32[648,128]{1,0:T(8,128)}, f32[162,128]{1,0:T(8,128)}) custom-call(bf16[96,384]{1,0:T(8,128)(2,1)S(1)} %bitcast.51, bf16[96,384]{1,0:T(8,128)(2,1)S(1)} %bitcast.52, bf16[112,384]{1,0:T(8,128)(2,1)S(1)} %bitcast.49, bf16[112,384]{1,0:T(8,128)(2,1)S(1)} %bitcast.50, bf16[64,384]{1,0:T(8,128)(2,1)S(1)} %bitcast.53, bf16[64,384]{1,0:T(8,128)(2,1)S(1)} %bitcast.54), custom_call_target="tpu_custom_call" | custom-call | tf_op jit(solution)/shard_map/finish/pallas_call | solution.py:34
  (38 shorter events, 3.1 us)
Async XLA Ops:
  2.7 7.1 %collective-permute-start = (bf16[272,384]{1,0:T(8,128)(2,1)}, bf16[272,384]{1,0:T(8,128)(2,1)S(1)}, u32[]{:S(2)}, u32[]{:S(2)}) collective-permute-start(bf16[272,384]{1,0:T(8,128)(2,1)} %get-tuple-element.59), channel_id=1, source_target_pairs={{0,1},{1,0},{2,3},{3,2},{4,5},{5,4},{6,7},{7,6},{8,9},{9,8},{10,11... | collective-permute-start | bytes 626696 | tf_op jit(solution)/shard_map/ppermute | solution.py:611
  3.2 6.5 %collective-permute-start.1 = (bf16[272,384]{1,0:T(8,128)(2,1)}, bf16[272,384]{1,0:T(8,128)(2,1)S(1)}, u32[]{:S(2)}, u32[]{:S(2)}) collective-permute-start(bf16[272,384]{1,0:T(8,128)(2,1)} %get-tuple-element.60), channel_id=1, source_target_pairs={{1,2},{2,1},{3,4},{4,3},{5,6},{6,5},{7,8},{8,7},{9,10},{10,9},{11,... | collective-permute-start | bytes 626696 | tf_op jit(solution)/shard_map/ppermute | solution.py:616
  3.9 14.9 %collective-permute-start.3 = (bf16[256,384]{1,0:T(8,128)(2,1)}, bf16[256,384]{1,0:T(8,128)(2,1)S(1)}, u32[]{:S(2)}, u32[]{:S(2)}) collective-permute-start(bf16[256,384]{1,0:T(8,128)(2,1)} %get-tuple-element.70), channel_id=1, source_target_pairs={{0,16},{16,0},{1,17},{17,1},{2,18},{18,2},{3,19},{19,3},{4,20},{20... | collective-permute-start | bytes 589832 | tf_op jit(solution)/shard_map/ppermute | solution.py:611
  6.4 1.5 %copy-start = (bf16[2,3,3,192,192]{4,3,2,1,0:T(8,128)(2,1)S(1)}, bf16[2,3,3,192,192]{4,3,2,1,0:T(8,128)(2,1)}, u32[]{:S(2)}) copy-start(bf16[2,3,3,192,192]{4,3,2,1,0:T(8,128)(2,1)} %param.12) | copy-start | bytes 3981316
  7.9 1.0 %copy-start.1 = (bf16[528,384]{1,0:T(8,128)(2,1)S(1)}, bf16[528,384]{1,0:T(8,128)(2,1)}, u32[]{:S(2)}) copy-start(bf16[528,384]{1,0:T(8,128)(2,1)} %get-tuple-element.57.own_in) | copy-start | bytes 1216516
  8.9 0.7 %copy-start.2 = (bf16[4,384]{1,0:T(4,128)(2,1)S(1)}, bf16[4,384]{1,0:T(4,128)(2,1)}, u32[]{:S(2)}) copy-start(bf16[4,384]{1,0:T(4,128)(2,1)} %coupling_ref.1) | copy-start | bytes 9220
  8.9 0.7 %copy-start.3 = (bf16[384,4]{0,1:T(4,128)(2,1)S(1)}, bf16[384,4]{0,1:T(4,128)(2,1)}, u32[]{:S(2)}) copy-start(bf16[384,4]{0,1:T(4,128)(2,1)} %param.16) | copy-start | bytes 9220
  8.9 0.7 %copy-start.4 = (bf16[4,192]{1,0:T(4,128)(2,1)S(1)}, bf16[4,192]{1,0:T(4,128)(2,1)}, u32[]{:S(2)}) copy-start(bf16[4,192]{1,0:T(4,128)(2,1)} %param.15) | copy-start | bytes 4612
  8.9 0.7 %copy-start.5 = (bf16[192,4]{0,1:T(4,128)(2,1)S(1)}, bf16[192,4]{0,1:T(4,128)(2,1)}, u32[]{:S(2)}) copy-start(bf16[192,4]{0,1:T(4,128)(2,1)} %param.14) | copy-start | bytes 4612
  10.0 3.7 %collective-permute-start.2 = (f32[4,512]{1,0:T(4,128)S(1)}, f32[4,512]{1,0:T(4,128)S(1)}, u32[]{:S(2)}, u32[]{:S(2)}) collective-permute-start(f32[4,512]{1,0:T(4,128)S(1)} %get-tuple-element.63.sent_ref), channel_id=1, source_target_pairs={{0,16},{16,0},{1,17},{17,1},{2,18},{18,2},{3,19},{19,3},{4,20},{20... | collective-permute-start | bytes 24584 | tf_op jit(solution)/shard_map/ppermute | solution.py:611
  12.0 6.8 %collective-permute-start.4 = (bf16[256,384]{1,0:T(8,128)(2,1)S(1)}, bf16[256,384]{1,0:T(8,128)(2,1)S(1)}, u32[]{:S(2)}, u32[]{:S(2)}) collective-permute-start(bf16[256,384]{1,0:T(8,128)(2,1)S(1)} %get-tuple-element.71), channel_id=1, source_target_pairs={{0,16},{16,0},{1,17},{17,1},{2,18},{18,2},{3,19},{19,3},{4,20},{20... | collective-permute-start | bytes 589832 | tf_op jit(solution)/shard_map/ppermute | solution.py:611
  15.9 7.7 %collective-permute-start.6 = (bf16[256,384]{1,0:T(8,128)(2,1)S(1)}, bf16[256,384]{1,0:T(8,128)(2,1)S(1)}, u32[]{:S(2)}, u32[]{:S(2)}) collective-permute-start(bf16[256,384]{1,0:T(8,128)(2,1)S(1)} %get-tuple-element.78), channel_id=1, source_target_pairs={{1,2},{2,1},{3,4},{4,3},{5,6},{6,5},{7,8},{8,7},{9,10},{10,9},{11,... | collective-permute-start | bytes 589832 | tf_op jit(solution)/shard_map/ppermute | solution.py:616
  16.5 5.9 %collective-permute-start.5 = (bf16[256,384]{1,0:T(8,128)(2,1)S(1)}, bf16[256,384]{1,0:T(8,128)(2,1)S(1)}, u32[]{:S(2)}, u32[]{:S(2)}) collective-permute-start(bf16[256,384]{1,0:T(8,128)(2,1)S(1)} %get-tuple-element.68.give_ref), channel_id=1, source_target_pairs={{0,16},{16,0},{1,17},{17,1},{2,18},{18,2},{3,19},{19,3},{4,20},{20... | collective-permute-start | bytes 589832 | tf_op jit(solution)/shard_map/ppermute | solution.py:611
  23.9 9.2 %collective-permute-start.7 = (bf16[8,304,384]{2,1,0:T(8,128)(2,1)S(1)}, bf16[8,304,384]{2,1,0:T(8,128)(2,1)S(1)}, u32[]{:S(2)}, u32[]{:S(2)}) collective-permute-start(bf16[8,304,384]{2,1,0:T(8,128)(2,1)S(1)} %chunk.2), channel_id=1, source_target_pairs={{0,1},{1,0},{2,3},{3,2},{4,5},{5,4},{6,7},{7,6},{8,9},{9,8},{10,11... | collective-permute-start | bytes 5603336 | tf_op jit(solution)/shard_map/ppermute | solution.py:611
  33.3 17.1 %collective-permute-start.10 = (bf16[4,1,96,384]{3,2,1,0:T(8,128)(2,1)S(1)}, bf16[4,1,96,384]{3,2,1,0:T(8,128)(2,1)S(1)}, u32[]{:S(2)}, u32[]{:S(2)}) collective-permute-start(bf16[4,1,96,384]{3,2,1,0:T(8,128)(2,1)S(1)} %get-tuple-element.89), channel_id=1, source_target_pairs={{0,2},{1,3},{2,0},{3,1},{4,6},{5,7},{6,4},{7,5},{8,10},{9,11},{10,... | collective-permute-start | bytes 884744 | tf_op jit(solution)/shard_map/ppermute | solution.py:611
  36.6 9.8 %collective-permute-start.9 = (bf16[2,2,112,384]{3,2,1,0:T(8,128)(2,1)S(1)}, bf16[2,2,112,384]{3,2,1,0:T(8,128)(2,1)S(1)}, u32[]{:S(2)}, u32[]{:S(2)}) collective-permute-start(bf16[2,2,112,384]{3,2,1,0:T(8,128)(2,1)S(1)} %get-tuple-element.84), channel_id=1, source_target_pairs={{0,4},{1,5},{2,6},{3,7},{4,0},{5,1},{6,2},{7,3},{8,12},{9,13},{10,... | collective-permute-start | bytes 1032200 | tf_op jit(solution)/shard_map/ppermute | solution.py:611
  39.6 4.0 %collective-permute-start.8 = (f32[4,256]{1,0:T(4,128)S(1)}, f32[4,256]{1,0:T(4,128)S(1)}, u32[]{:S(2)}, u32[]{:S(2)}) collective-permute-start(f32[4,256]{1,0:T(4,128)S(1)} %get-tuple-element.82), channel_id=1, source_target_pairs={{0,16},{16,0},{1,17},{17,1},{2,18},{18,2},{3,19},{19,3},{4,20},{20... | collective-permute-start | bytes 12296 | tf_op jit(solution)/shard_map/ppermute | solution.py:611
  41.6 9.3 %collective-permute-start.13 = (bf16[4,1,64,384]{3,2,1,0:T(8,128)(2,1)S(1)}, bf16[4,1,64,384]{3,2,1,0:T(8,128)(2,1)S(1)}, u32[]{:S(2)}, u32[]{:S(2)}) collective-permute-start(bf16[4,1,64,384]{3,2,1,0:T(8,128)(2,1)S(1)} %get-tuple-element.96), channel_id=1, source_target_pairs={{0,2},{1,3},{2,0},{3,1},{4,6},{5,7},{6,4},{7,5},{8,10},{9,11},{10,... | collective-permute-start | bytes 589832 | tf_op jit(solution)/shard_map/ppermute | solution.py:611
  46.6 12.1 %collective-permute-start.12 = (bf16[1,2,112,384]{3,2,1,0:T(8,128)(2,1)S(1)}, bf16[1,2,112,384]{3,2,1,0:T(8,128)(2,1)S(1)}, u32[]{:S(2)}, u32[]{:S(2)}) collective-permute-start(bf16[1,2,112,384]{3,2,1,0:T(8,128)(2,1)S(1)} %get-tuple-element.94), channel_id=1, source_target_pairs={{0,8},{1,9},{2,10},{3,11},{4,12},{5,13},{6,14},{7,15},{8,0},{9,1},... | collective-permute-start | bytes 516104 | tf_op jit(solution)/shard_map/ppermute | solution.py:611
  50.5 8.2 %collective-permute-start.11 = (bf16[2,1,96,384]{3,2,0,1:T(8,128)(2,1)S(1)}, bf16[2,1,96,384]{3,2,0,1:T(8,128)(2,1)S(1)}, u32[]{:S(2)}, u32[]{:S(2)}) collective-permute-start(bf16[2,1,96,384]{3,2,0,1:T(8,128)(2,1)S(1)} %bitcast.55), channel_id=1, source_target_pairs={{0,4},{1,5},{2,6},{3,7},{4,0},{5,1},{6,2},{7,3},{8,12},{9,13},{10,... | collective-permute-start | bytes 442376 | tf_op jit(solution)/shard_map/ppermute | solution.py:611
  50.9 9.2 %collective-permute-start.16 = (bf16[2,1,64,384]{3,2,0,1:T(8,128)(2,1)S(1)}, bf16[2,1,64,384]{3,2,0,1:T(8,128)(2,1)S(1)}, u32[]{:S(2)}, u32[]{:S(2)}) collective-permute-start(bf16[2,1,64,384]{3,2,0,1:T(8,128)(2,1)S(1)} %bitcast.56), channel_id=1, source_target_pairs={{0,4},{1,5},{2,6},{3,7},{4,0},{5,1},{6,2},{7,3},{8,12},{9,13},{10,... | collective-permute-start | bytes 294920 | tf_op jit(solution)/shard_map/ppermute | solution.py:611
  58.8 6.8 %collective-permute-start.15 = (bf16[1,1,112,384]{3,2,1,0:T(8,128)(2,1)S(1)}, bf16[1,1,112,384]{3,2,1,0:T(8,128)(2,1)S(1)}, u32[]{:S(2)}, u32[]{:S(2)}) collective-permute-start(bf16[1,1,112,384]{3,2,1,0:T(8,128)(2,1)S(1)} %get-tuple-element.102), channel_id=1, source_target_pairs={{0,2},{1,3},{2,0},{3,1},{4,6},{5,7},{6,4},{7,5},{8,10},{9,11},{10,... | collective-permute-start | bytes 258056 | tf_op jit(solution)/shard_map/ppermute | solution.py:611
  59.5 6.1 %collective-permute-start.14 = (bf16[1,1,96,384]{3,2,1,0:T(8,128)(2,1)S(1)}, bf16[1,1,96,384]{3,2,1,0:T(8,128)(2,1)S(1)}, u32[]{:S(2)}, u32[]{:S(2)}) collective-permute-start(bf16[1,1,96,384]{3,2,1,0:T(8,128)(2,1)S(1)} %get-tuple-element.100), channel_id=1, source_target_pairs={{0,8},{1,9},{2,10},{3,11},{4,12},{5,13},{6,14},{7,15},{8,0},{9,1},... | collective-permute-start | bytes 221192 | tf_op jit(solution)/shard_map/ppermute | solution.py:611
  60.1 5.5 %collective-permute-start.17 = (bf16[1,1,64,384]{3,2,1,0:T(8,128)(2,1)S(1)}, bf16[1,1,64,384]{3,2,1,0:T(8,128)(2,1)S(1)}, u32[]{:S(2)}, u32[]{:S(2)}) collective-permute-start(bf16[1,1,64,384]{3,2,1,0:T(8,128)(2,1)S(1)} %get-tuple-element.107), channel_id=1, source_target_pairs={{0,8},{1,9},{2,10},{3,11},{4,12},{5,13},{6,14},{7,15},{8,0},{9,1},... | collective-permute-start | bytes 147464 | tf_op jit(solution)/shard_map/ppermute | solution.py:611
